TPU v7x, 256 devices: a whole 4x4x8 slice. The times are simulated.
256 devices in a mesh: dp: 16 (over y, z_hi), tensor: 16 (over z_lo, x, core).
Axes of the slice: x: 4, y: 4, z: 8 (z_hi: 4, z_lo: 2; z = z_hi * 2 + z_lo), core: 2. Of those that a mesh axis runs over, the one named last changes fastest.
Arguments:
- tokens_in: bfloat16 [2, 384, 5120], P(None, 'dp'), may hold values from -6 to 6
- attn_gain: float32 [5120], replicated, may hold values from 0.5 to 1.5
- post_gain: float32 [5120], replicated, may hold values from 0.5 to 1.5
- w_query: bfloat16 [5120, 4096], P(None, 'tensor'), may hold values from -0.078125 to 0.078125
- key_weight_base: bfloat16 [5120, 2048], P(None, 'tensor'), may hold values from -0.078125 to 0.078125
- value_weight_base: bfloat16 [5120, 2048], P(None, 'tensor'), may hold values from -0.078125 to 0.078125
- w_out: bfloat16 [4096, 5120], P('tensor'), may hold values from -0.09375 to 0.09375
- left_qkv: float32 [3, 5120, 64], P(None, 'dp'), may hold values from -0.078125 to 0.078125
- right_query: float32 [64, 4096], P('dp', 'tensor'), may hold values from -0.75 to 0.75
- right_key_value: float32 [2, 64, 2048], P(None, 'dp', 'tensor'), may hold values from -0.75 to 0.75
- left_out: float32 [4096, 64], P('tensor', 'dp'), may hold values from -0.09375 to 0.09375
- right_out: float32 [64, 5120], P('dp'), may hold values from -0.75 to 0.75
- kv_cache: bfloat16 [2, 384, 16, 320, 128], P(None, 'dp', 'tensor'), may hold values from -410 to 410
- lengths: int32 [384], P('dp'), may hold values from 1 to 320, as said below
- starts: int32 [384], P('dp'), may hold values from 0 to 319
Outputs:
- hidden_out: bfloat16 [2, 384, 5120], P(None, 'dp')
- mlp_input: bfloat16 [2, 384, 5120], P(None, 'dp')
- new_kv: bfloat16 [2, 2, 384, 2048], P(None, None, 'dp', 'tensor')
Inputs may be any that keep to these rules, and one draw needn't show every extreme that they name: `lengths`: some rollout has exactly 320 cached tokens.
All inputs are finite; a program needn't handle non-finite values.
Results may differ from a plain program's by a relative error of at most 0.012.
The roundings to bfloat16 on the way count: a program that leaves them out, or rounds other values in their place, can miss the bound.
Values may be sent and summed in bfloat16 or wider, within the bound.
A program may use at most 128 MiB of HBM per device.

v0:
```python
import math

import jax
import jax.numpy as jnp
from jax import lax
from jax.sharding import PartitionSpec as P

MODEL_WIDTH = 5120
HEAD_WIDTH = 128
WINDOW = 256


ROPE_BASE = 1000000.0


def apply_rotary(vectors, token_positions):
    half_size = vectors.shape[-1] // 2
    inverse_freq = ROPE_BASE ** (
        -(jnp.arange(half_size, dtype=jnp.float32) * 2.0 / vectors.shape[-1])
    )
    angles = token_positions.astype(jnp.float32)[:, None] * inverse_freq[None, :]
    cosine = jnp.cos(angles)[:, None, :]
    sine_part = jnp.sin(angles)[:, None, :]
    lower_half = vectors[..., :half_size]
    upper_half = vectors[..., half_size:]
    return jnp.concatenate(
        [
            lower_half * cosine - upper_half * sine_part,
            upper_half * cosine + lower_half * sine_part,
        ],
        -1,
    )


def normalize(values, gains):
    return values * lax.rsqrt(jnp.mean(values * values, -1, keepdims=True) + 1e-06) * gains


def attend(
    queries, cache_keys, cache_vals, fresh_keys, fresh_vals, lengths, starts, token_positions
):
    batch_rows, head_count, head_size = queries.shape
    kv_count = cache_keys.shape[1]
    slot_count = cache_keys.shape[2]
    grouped = queries.reshape(batch_rows, kv_count, head_count // kv_count, head_size)
    scale_factor = 1.0 / math.sqrt(head_size)
    cached_scores = (
        jnp.einsum("bkgd,bkcd->bkgc", grouped, cache_keys, preferred_element_type=jnp.float32)
        * scale_factor
    )
    fresh_scores = (
        jnp.einsum("bkgd,bked->bkge", grouped, fresh_keys, preferred_element_type=jnp.float32)
        * scale_factor
    )
    slot_ids = jnp.arange(slot_count, dtype=jnp.int32)
    logical = (slot_ids[None, :] - starts[:, None]) % slot_count
    visible = (logical < lengths[:, None]) & (token_positions[:, None] - logical < WINDOW)
    cached_scores = jnp.where(visible[:, None, None, :], cached_scores, -1e30)
    row_max = jnp.maximum(
        jnp.max(cached_scores, -1, keepdims=True), jnp.max(fresh_scores, -1, keepdims=True)
    )
    cached_exp = jnp.exp(cached_scores - row_max)
    fresh_exp = jnp.exp(fresh_scores - row_max)
    denominator = jnp.sum(cached_exp, -1, keepdims=True) + jnp.sum(fresh_exp, -1, keepdims=True)
    cached_prob = (cached_exp / denominator).astype(jnp.bfloat16)
    fresh_prob = (fresh_exp / denominator).astype(jnp.bfloat16)
    blended = jnp.einsum(
        "bkgc,bkcd->bkgd", cached_prob, cache_vals, preferred_element_type=jnp.float32
    )
    blended = blended + jnp.einsum(
        "bkge,bked->bkgd", fresh_prob, fresh_vals, preferred_element_type=jnp.float32
    )
    return blended.reshape(batch_rows, head_count * head_size).astype(jnp.bfloat16)


def shards(
    tokens_in,
    attn_gain,
    post_gain,
    w_query,
    key_weight_base,
    value_weight_base,
    w_out,
    left_qkv,
    right_query,
    right_key_value,
    left_out,
    right_out,
    kv_cache,
    lengths,
    starts,
):
    gathered_rq, gathered_rkv, gathered_ro, gathered_lo = (
        lax.all_gather(right_query, "dp", axis=0, tiled=True),
        lax.all_gather(right_key_value, "dp", axis=1, tiled=True),
        lax.all_gather(right_out, "dp", axis=0, tiled=True),
        lax.all_gather(left_out, "dp", axis=1, tiled=True),
    )
    query_cols = w_query.shape[1]
    key_cols = key_weight_base.shape[1]
    piece = lax.all_gather(left_qkv, "dp", axis=1, tiled=True)
    merged_parts = []
    pairs = (
        (w_query, gathered_rq),
        (key_weight_base, gathered_rkv[0]),
        (value_weight_base, gathered_rkv[1]),
    )
    for index_num in range(3):
        base_weight, right_part = pairs[index_num]
        base_rows = base_weight.astype(jnp.float32)
        update = jnp.dot(piece[index_num], right_part, precision=lax.Precision.HIGHEST)
        merged_parts.append(base_rows + 0.5 * update)
    merged = jnp.concatenate(merged_parts, 1).astype(jnp.bfloat16)
    out_update = jnp.dot(gathered_lo, gathered_ro, precision=lax.Precision.HIGHEST)
    merged_out = (w_out.astype(jnp.float32) + 0.5 * out_update).astype(jnp.bfloat16)
    batch_rows = tokens_in.shape[1]
    inputs = tokens_in.astype(jnp.float32)
    normalized_input = (
        normalize(inputs, attn_gain).astype(jnp.bfloat16).reshape(2 * batch_rows, MODEL_WIDTH)
    )
    projected = jnp.dot(normalized_input, merged, preferred_element_type=jnp.float32)
    query_heads = query_cols // HEAD_WIDTH
    kv_heads = key_cols // HEAD_WIDTH
    fresh_keys = []
    fresh_vals = []
    attended_list = []
    key_value_list = []
    for token_step in range(2):
        step_rows = projected[token_step * batch_rows : (token_step + 1) * batch_rows]
        token_positions = lengths + token_step
        queries = apply_rotary(
            step_rows[:, :query_cols].reshape(batch_rows, query_heads, HEAD_WIDTH), token_positions
        ).astype(jnp.bfloat16)
        incoming_keys = apply_rotary(
            step_rows[:, query_cols : query_cols + key_cols].reshape(
                batch_rows, kv_heads, HEAD_WIDTH
            ),
            token_positions,
        ).astype(jnp.bfloat16)
        incoming_values = (
            step_rows[:, query_cols + key_cols :]
            .reshape(batch_rows, kv_heads, HEAD_WIDTH)
            .astype(jnp.bfloat16)
        )
        fresh_keys.append(incoming_keys)
        fresh_vals.append(incoming_values)
        attended_list.append(
            attend(
                queries,
                kv_cache[0],
                kv_cache[1],
                jnp.stack(fresh_keys, 2),
                jnp.stack(fresh_vals, 2),
                lengths,
                starts,
                token_positions,
            )
        )
        key_value_list.append(
            jnp.stack(
                [
                    incoming_keys.reshape(batch_rows, key_cols),
                    incoming_values.reshape(batch_rows, key_cols),
                ]
            )
        )
    attended = jnp.concatenate(attended_list, 0)
    partial_value = jnp.dot(attended, merged_out, preferred_element_type=jnp.float32).reshape(
        2, batch_rows, MODEL_WIDTH
    )
    summed = lax.psum(partial_value, "tensor")
    hidden_out = (inputs + summed).astype(jnp.bfloat16)
    mlp_input = normalize(hidden_out.astype(jnp.float32), post_gain).astype(jnp.bfloat16)
    return (hidden_out, mlp_input, jnp.stack(key_value_list))


def solution(mesh):
    in_specs = (
        P(None, "dp", None),
        P(),
        P(),
        P(None, "tensor"),
        P(None, "tensor"),
        P(None, "tensor"),
        P("tensor", None),
        P(None, "dp", None),
        P("dp", "tensor"),
        P(None, "dp", "tensor"),
        P("tensor", "dp"),
        P("dp", None),
        P(None, "dp", "tensor", None, None),
        P("dp"),
        P("dp"),
    )
    out_specs = (P(None, "dp", None), P(None, "dp", None), P(None, None, "dp", "tensor"))
    return jax.shard_map(shards, mesh=mesh, in_specs=in_specs, out_specs=out_specs, check_vma=False)
```

profile of v0, /device:TPU:1, one launch (start us, length us, event | category | flops | bytes accessed | tf_op | source)
XLA Modules:
  0.0 372.7 jit_solution(14624067556203179335)
XLA Ops:
  7.3 0.7 all-gather.8.cloned.1.call-update
  8.0 2.1 copy.23
  10.1 0.7 copy.24
  10.8 41.1 %all-gather = f32[16,4,256]{2,1,0:T(4,128)S(1)} all-gather(f32[1,4,256]{2,1,0:T(4,128)} %bitcast.118), channel_id=1, replica_groups=mesh['dp'=16,'tensor'=16] {'dp'}, dimensions={0}, use_global_device_ids=true | all-gather | bytes 69632 | tf_op jit(solution)/shard_map/all_gather | solution.py:94
  51.9 32.6 %all-gather.1 = f32[16,4,256]{2,1,0:T(4,128)S(1)} all-gather(f32[1,4,256]{2,1,0:T(4,128)} %bitcast.119), channel_id=1, replica_groups=mesh['dp'=16,'tensor'=16] {'dp'}, dimensions={0}, use_global_device_ids=true | all-gather | bytes 69632 | tf_op jit(solution)/shard_map/all_gather | solution.py:97
  84.6 36.5 %all_gather.17 = f32[2,64,128]{2,0,1:T(2,128)S(1)} all-gather(f32[2,4,128]{2,0,1:T(2,128)S(1)} %copy.24), channel_id=1, replica_groups=mesh['dp'=16,'tensor'=16] {'dp'}, dimensions={1}, use_global_device_ids=true | all-gather | bytes 69632 | tf_op jit(solution)/shard_map/all_gather | solution.py:95
  121.2 1.2 fusion.29
  122.8 1.0 fusion.31
  123.7 2.8 reshape.641
  126.5 6.4 %fusion.2 = bf16[256,5120]{1,0:T(8,128)(2,1)S(1)} fusion(f32[64,256]{1,0:T(8,128)S(1)} %reshape.639, f32[64,5120]{1,0:T(8,128)} %reshape.641, bf16[256,5120]{1,0:T(8,128)(2,1)} %param.21), kind=kOutput, calls=%fused_computation.4 | convolution fusion | flops 1011875840 | bytes 6619136 | tf_op jit(solution)/shard_map/dot_general | solution.py:114
  133.0 60.8 %all-gather.6.cloned.1.call-done = f32[3,5120,64]{2,0,1:T(4,128)} async-done(((f32[3,320,64]{2,0,1:T(4,128)}), f32[3,5120,64]{2,0,1:T(4,128)}) %all-gather.6.cloned.1.call-update) | async-done | bytes 3932176 | tf_op jit(solution)/shard_map/all_gather | solution.py:101
  193.8 16.7 %fusion.77 = (f32[1,5120,64]{2,0,1:T(1,128)S(1)}, f32[1,5120,64]{2,0,1:T(1,128)S(1)}, f32[1,5120,64]{2,0,1:T(1,128)S(1)}) fusion(f32[3,5120,64]{2,0,1:T(4,128)} %all-gather.6.cloned.1.call-done), kind=kLoop, calls=%fused_computation.134 | loop fusion | bytes 7864320 | tf_op jit(solution)/shard_map/slice | solution.py:111
  210.5 2.2 fusion.6
  212.7 2.2 fusion.7
  215.0 4.6 %fusion.3 = bf16[5120,256]{1,0:T(8,128)(2,1)S(1)} fusion(f32[5120,64]{1,0:T(8,128)S(1)} %bitcast.96, f32[64,256]{1,0:T(8,128)S(1)} %reshape.637, bf16[5120,256]{1,0:T(8,128)(2,1)S(1)} %copy-done.1), kind=kOutput, calls=%fused_computation.5 | convolution fusion | flops 1011875840 | bytes 6619136 | tf_op jit(solution)/shard_map/dot_general | solution.py:111
  219.6 1.1 fusion.80
  221.4 2.6 fusion.83
  224.2 2.0 fusion.25
  226.6 0.8 fusion.81
  228.5 1.6 fusion.45
  230.2 0.6 pad_maximum_fusion
  230.8 133.0 %all-reduce.2.cloned.1.call-done = f32[2,24,5120]{2,1,0:T(8,128)} async-done(((f32[2,24,5120]{2,1,0:T(8,128)}), f32[2,24,5120]{2,1,0:T(8,128)}) %all-reduce.2.cloned.1.call-update) | async-done | bytes 983056 | tf_op jit(solution)/shard_map/psum | solution.py:171
  363.8 1.4 fusion.26
  365.2 1.0 fusion.28
  (61 shorter events, 2.9 us)
Async XLA Ops:
  7.2 115.6 %copy-start = (bf16[2,24,5120]{2,1,0:T(8,128)(2,1)S(1)}, bf16[2,24,5120]{2,1,0:T(8,128)(2,1)}, u32[]{:S(2)}) copy-start(bf16[2,24,5120]{2,1,0:T(8,128)(2,1)} %param.15) | copy-start | bytes 1474564
  7.2 115.2 %copy-start.8 = (s32[24]{0:T(128)S(1)}, s32[24]{0:T(128)}, u32[]{:S(2)}) copy-start(s32[24]{0:T(128)} %param.28) | copy-start | bytes 292
  7.2 115.2 %copy-start.9 = (s32[24]{0:T(128)S(1)}, s32[24]{0:T(128)}, u32[]{:S(2)}) copy-start(s32[24]{0:T(128)} %param.29) | copy-start | bytes 292
  7.2 115.6 %copy-start.6 = (f32[5120]{0:T(1024)S(1)}, f32[5120]{0:T(1024)}, u32[]{:S(2)}) copy-start(f32[5120]{0:T(1024)} %param.16) | copy-start | bytes 61444
  7.2 116.5 %all-gather.8.cloned.1.call-start = ((), (), s32[]{:S(2)}) async-start(), calls=%async_computation.2 | async-start | bytes 1392640 | tf_op jit(solution)/shard_map/all_gather | solution.py:96
  7.9 185.8 %all-gather.6.cloned.1.call-start = ((), (), s32[]{:S(2)}) async-start(), calls=%async_computation | async-start | bytes 11141120 | tf_op jit(solution)/shard_map/all_gather | solution.py:101
  10.1 353.7 %all-reduce.2.cloned.1.call-start = ((), (), s32[]{:S(2)}) async-start(), calls=%async_computation.1 | async-start | bytes 1966080 | tf_op jit(solution)/shard_map/psum | solution.py:171
  193.8 16.7 %copy-start.3 = (bf16[5120,128]{1,0:T(8,128)(2,1)S(1)}, bf16[5120,128]{1,0:T(8,128)(2,1)}, u32[]{:S(2)}) copy-start(bf16[5120,128]{1,0:T(8,128)(2,1)} %param.19) | copy-start | bytes 3932164
  210.5 2.2 copy-start.4
  212.7 2.2 copy-start.1
  215.0 4.7 %copy-start.5 = (bf16[2,24,5120]{2,1,0:T(8,128)(2,1)S(1)}, bf16[2,24,5120]{2,1,0:T(8,128)(2,1)}, u32[]{:S(2)}) copy-start(bf16[2,24,5120]{2,1,0:T(8,128)(2,1)} %fusion.31) | copy-start | bytes 1474564
  221.4 5.2 %copy-start.10 = (bf16[2,24,1,320,128]{4,3,2,1,0:T(8,128)(2,1)S(1)}, bf16[2,24,1,320,128]{4,3,2,1,0:T(8,128)(2,1)}, u32[]{:S(2)}) copy-start(bf16[2,24,1,320,128]{4,3,2,1,0:T(8,128)(2,1)} %param.27) | copy-start | bytes 11796484
  228.5 136.7 %copy-start.7 = (f32[5120]{0:T(1024)S(1)}, f32[5120]{0:T(1024)}, u32[]{:S(2)}) copy-start(f32[5120]{0:T(1024)} %param.17) | copy-start | bytes 61444
  365.2 1.0 copy-start.2
Sparse Core Ops, SparseCore 0:
  10.5 58.2 all-gather.7
  71.3 122.3 all-gather.5
  230.2 133.5 all-reduce.1
where the time goes:
time: 376 us; the launch traced here: 373 us
  waiting for transfers between devices  194 us (52%)
  blocking collectives  110 us (29%)
  matrix products  24.8 us (7%)
  local copies, waits for them, and re-layouts  22.4 us (6%)
  between operations  14.1 us (4%)
  other arithmetic  6.54 us (2%)
    psum x1, waiting for transfers between devices, shards(): summed = lax.psum(partial_value, 'tensor')  133 us
    all_gather x1, waiting for transfers between devices, shards(): piece = lax.all_gather(left_qkv, 'dp', axis=1, tiled=True)  60.8 us
    all_gather x1, blocking collectives, shards(): lax.all_gather(right_query, 'dp', axis=0, tiled=True)  41.1 us
    all_gather x1, blocking collectives, shards(): lax.all_gather(right_key_value, 'dp', axis=1, tiled=True)  36.5 us
    all_gather x1, blocking collectives, shards(): lax.all_gather(left_out, 'dp', axis=1, tiled=True)  32.6 us
    slice x1, local copies, waits for them, and re-layouts, shards(): piece[index_num]  16.7 us
    dot_general x3, matrix products, shards(): jnp.dot(piece[index_num], right_part, precision=lax.Precision.HIGHEST)  9.09 us
  transfers between devices with their start and end apart: 3, of which 2 were waited for; matrix products, arithmetic and copies ran while one was open for 4% of the time, Pallas kernels for 0%

commit v1 on v0

v1 whole, which is shorter than its diff:
```python
import math

import jax
import jax.numpy as jnp
from jax import lax
from jax.experimental import pallas as pl
from jax.experimental.pallas import tpu as pltpu
from jax.sharding import PartitionSpec as P

MESH = pl.DeviceIdType.MESH
BF16 = jnp.bfloat16
F32 = jnp.float32

WIDTH = 5120
HEAD = 128
SLOTS = 320
WINDOW = 256
RANK = 64
ROWS = 24
DP = 16
TP = 16
CHIPS = 8
BLOCK = WIDTH // CHIPS
LROWS = WIDTH // DP
LPAD = 384
NT = (((1,), (1,)), ((), ()))
TN = (((0,), (0,)), ((), ()))
NN = (((1,), (0,)), ((), ()))


def dot(a, b, dims=NN):
    return lax.dot_general(a, b, dims, preferred_element_type=F32)


def iota(shape, axis):
    return lax.broadcasted_iota(jnp.int32, shape, axis)


def one_hot(cond):
    return jnp.where(cond, 1.0, 0.0).astype(BF16)


def main_kernel(
    tok_in, gain_in, wq_in, wk_in, wv_in, wo_in, lqkv_in, rq_in, rkv_in, lo_in, ro_in, kv_in,
    len_in, start_in,
    hid_out, kv_out,
    tok, gain, w, wo, kvc, lens, starts,
    lbuf, rq, rkv, lob, rob,
    lsend, lgat, pack, pkgat, zgat, rmat,
    normed, proj, qs, kx, vx, score, prob, att, att2,
    ybuf, ysend, yrecv, yall, keep, bsend, brecv, csend, crecv, hid,
    loc, lsend_sem, lrecv_sem, psend_sem, precv_sem, zsend_sem, zrecv_sem,
    ysend_sem, yrecv_sem, y2send_sem, y2recv_sem, bsend_sem, brecv_sem, csend_sem, crecv_sem,
    gsend_sem, grecv_sem, fsend_sem, frecv_sem,
):
    dp = lax.axis_index("dp")
    tp = lax.axis_index("tensor")
    chip = tp // 2
    core = tp % 2
    sib = tp + 1 - 2 * core
    other = 1 - core

    def load(src, dst, k):
        c = pltpu.make_async_copy(src, dst, loc.at[k])
        c.start()
        return c

    active = jnp.logical_or(tp < 8, core == 0)
    slab = jnp.where(tp < 8, tp, tp // 2 + 4)
    shift = 64 * (dp % 2)
    lbuf[0:64, :] = jnp.zeros((64, RANK), F32)
    lbuf[LROWS:LPAD, :] = jnp.zeros((LPAD - LROWS, RANK), F32)
    ld_l = load(lqkv_in.at[slab // 4], lbuf.at[pl.ds(pl.multiple_of(shift, 64), LROWS)], 0)
    ld_rq = load(rq_in, rq, 1)
    ld_rkv = load(rkv_in, rkv, 2)
    ld_lo = load(lo_in, lob, 3)
    ld_ro = load(ro_in.at[:, pl.ds(pl.multiple_of(chip * BLOCK, 128), BLOCK)], rob, 4)
    ld_tok = load(tok_in, tok, 5)
    ld_gain = load(gain_in, gain, 6)
    ld_len = load(len_in, lens, 7)
    ld_st = load(start_in, starts, 8)
    ld_w = []
    step = WIDTH // 4
    for i in range(4):
        rs = pl.ds(i * step, step)
        ld_w.append([
            load(wq_in.at[rs], w.at[rs, 0:256], 9 + 3 * i),
            load(wk_in.at[rs], w.at[rs, 256:384], 10 + 3 * i),
            load(wv_in.at[rs], w.at[rs, 384:512], 11 + 3 * i),
        ])
    ld_k = load(kv_in.at[0, :, 0], kvc.at[0], 21)
    ld_v = load(kv_in.at[1, :, 0], kvc.at[1], 22)
    ld_wo = load(wo_in, wo, 23)

    barrier = pltpu.get_barrier_semaphore()

    def greet(d, _):
        pl.semaphore_signal(
            barrier, inc=1, device_id={"dp": (dp + d) % DP}, device_id_type=MESH)
        pl.semaphore_signal(
            barrier, inc=1, device_id={"tensor": (tp + d) % TP}, device_id_type=MESH)
        return 0

    lax.fori_loop(1, DP, greet, 0)

    ld_l.wait()
    pick = one_hot(iota((16, RANK), 1) == iota((16, RANK), 0) + 16 * (slab % 4))
    lsend[...] = dot(pick, lbuf[...].astype(BF16), NT).astype(BF16)
    lgat[dp] = lsend[...]
    ld_rq.wait()
    ld_rkv.wait()
    ld_lo.wait()
    ld_ro.wait()
    eye = one_hot(iota((8, 4), 0) == iota((8, 4), 1))
    lot = dot(eye, lob[...].astype(BF16), NT)[0:4]
    tiles = [rq[:, 0:128], rq[:, 128:256], rkv[0], rkv[1], lot[:, 0:128], lot[:, 128:256]]
    tiles += [rob[:, 128 * i : 128 * (i + 1)] for i in range(5)]
    tiles += [jnp.zeros((4, 128), F32)]
    pack[...] = jnp.concatenate(tiles, 0).astype(BF16)
    pkgat[dp] = pack[...]

    pl.semaphore_wait(barrier, 2 * (DP - 1))

    def lcopy(d):
        to = (dp + d) % DP
        return pltpu.make_async_remote_copy(
            lsend, lgat.at[dp], lsend_sem.at[d], lrecv_sem.at[dp],
            device_id={"dp": to}, device_id_type=MESH)

    def pcopy(d):
        to = (dp + d) % DP
        return pltpu.make_async_remote_copy(
            pack, pkgat.at[dp], psend_sem.at[d], precv_sem.at[dp],
            device_id={"dp": to}, device_id_type=MESH)

    def send_l(d, _):
        lcopy(d).start()
        return 0

    def send_p(d, _):
        pcopy(d).start()
        return 0

    @pl.when(active)
    def _():
        lax.fori_loop(1, DP, send_l, 0)

    lax.fori_loop(1, DP, send_p, 0)

    ld_tok.wait()
    ld_gain.wait()
    sq = jnp.zeros((2, ROWS, 1), F32)
    for i in range(8):
        v = tok[:, :, i * 640 : (i + 1) * 640].astype(F32)
        sq = sq + jnp.sum(v * v, -1, keepdims=True)
    rs = lax.rsqrt(sq * (1.0 / WIDTH) + 1e-06)
    for i in range(8):
        cols = slice(i * 640, (i + 1) * 640)
        v = tok[:, :, cols].astype(F32) * rs * gain[:, cols][None]
        normed[:, cols] = v.reshape(2 * ROWS, 640).astype(BF16)

    acc = None
    for i in range(2):
        for c in ld_w[i]:
            c.wait()
        part = dot(normed[:, i * step : (i + 1) * step], w[i * step : (i + 1) * step, :])
        acc = part if acc is None else acc + part
    proj[...] = acc

    def zcopy(d, to, src, who):
        return pltpu.make_async_remote_copy(
            zgat.at[src], zgat.at[src], zsend_sem.at[d], zrecv_sem.at[src],
            device_id={"tensor": to}, device_id_type=MESH)

    @pl.when(active)
    def _():
        def got(d, _):
            src = (dp + d) % DP
            pltpu.make_async_copy(lgat.at[src], lgat.at[src], lrecv_sem.at[src]).wait()
            return 0

        lax.fori_loop(1, DP, got, 0)
        z = jnp.zeros((16, 2 * ROWS), F32)
        for j in range(DP):
            base = 640 * (j // 2) + 256 * (j % 2)
            z = z + dot(lgat[j], normed[:, base : base + LPAD], NT)
        z = jnp.concatenate([z, jnp.zeros((16, 128 - 2 * ROWS), F32)], 1)
        zgat[slab] = z.astype(BF16)

        def send_z(d, _):
            zcopy(d, (tp + d) % TP, slab, tp).start()
            return 0

        lax.fori_loop(1, TP, send_z, 0)

    acc = proj[...]
    for i in range(2, 4):
        for c in ld_w[i]:
            c.wait()
        acc = acc + dot(normed[:, i * step : (i + 1) * step], w[i * step : (i + 1) * step, :])
    proj[...] = acc

    ld_len.wait()
    ld_st.wait()
    lenf = lens[...].astype(F32)
    stf = starts[...].astype(F32)

    def column(values, rows, owner):
        hit = owner(iota((rows, ROWS), 0)) == iota((rows, ROWS), 1)
        return jnp.sum(jnp.where(hit, values, 0.0), -1, keepdims=True)

    row = iota((2 * ROWS, 1), 0)
    pos = column(lenf, 2 * ROWS, lambda r: r % ROWS) + jnp.where(row >= ROWS, 1.0, 0.0)
    lane = iota((1, HEAD), 1)
    freq = jnp.exp((lane % 64).astype(F32) * (-2.0 * math.log(1000000.0) / HEAD))
    angle = pos * freq
    cos = jnp.cos(angle)
    sin = jnp.sin(angle) * jnp.where(lane < 64, -1.0, 1.0)

    def rope(v):
        return v * cos + pltpu.roll(v, 64, 1) * sin

    arow = iota((4 * ROWS, 1), 0)
    tokstep = jnp.where(arow % 4 >= 2, 1.0, 0.0)
    alen = column(lenf, 4 * ROWS, lambda r: r // 4)
    ast = column(stf, 4 * ROWS, lambda r: r // 4)
    slot = iota((4 * ROWS, SLOTS), 1).astype(F32) - ast
    slot = jnp.where(slot < 0, slot + float(SLOTS), slot)
    visible = jnp.logical_and(slot < alen, alen + tokstep - slot < float(WINDOW))

    def gotp(d, _):
        src = (dp + d) % DP
        pltpu.make_async_copy(pkgat.at[src], pkgat.at[src], precv_sem.at[src]).wait()
        return 0

    lax.fori_loop(1, DP, gotp, 0)
    o = iota((256, 256), 0)
    perm = one_hot(iota((256, 256), 1) == ((o % 64) // 4) * 16 + 4 * (o // 64) + o % 4)
    for g in range(3):
        grp = pkgat[:, 16 * g : 16 * (g + 1), :].reshape(256, 128)
        rmat[g] = dot(perm, grp).astype(BF16)

    def gotz(s, _):
        src = jnp.where(s < 8, s, 2 * s - 8)

        @pl.when(src != tp)
        def _():
            pltpu.make_async_copy(zgat.at[s], zgat.at[s], zrecv_sem.at[s]).wait()

        return 0

    lax.fori_loop(0, 12, gotz, 0)
    cols = []
    for t, p in enumerate((0, 0, 1, 2)):
        z = zgat[4 * p : 4 * (p + 1)].reshape(RANK, 128)
        delta = dot(z, rmat[0, 64 * t : 64 * (t + 1), :], TN)[: 2 * ROWS]
        cols.append(proj[:, 128 * t : 128 * (t + 1)] + 0.5 * delta)
    rounded = [rope(cols[0]), rope(cols[1]), rope(cols[2]), cols[3]]
    rounded = [v.astype(BF16).astype(F32) for v in rounded]
    for t in range(2):
        rows = slice(t * ROWS, (t + 1) * ROWS)
        kv_out[t, 0] = rounded[2][rows].astype(BF16)
        kv_out[t, 1] = rounded[3][rows].astype(BF16)
        for g in range(2):
            qs[pl.ds(2 * t + g, ROWS, stride=4), :] = rounded[g][rows]
        for r in range(4):
            kx[t, pl.ds(r, ROWS, stride=4), :] = rounded[2][rows]
            vx[t, pl.ds(r, ROWS, stride=4), :] = rounded[3][rows]

    scale = 1.0 / math.sqrt(HEAD)
    ld_k.wait()
    which = iota((16, 1), 0) // 4
    for i in range(6):
        q = qs[16 * i : 16 * (i + 1), :].astype(BF16)
        s = dot(q, kvc[0, 4 * i], NT)
        for b in range(1, 4):
            s = jnp.where(which == b, dot(q, kvc[0, 4 * i + b], NT), s)
        score[16 * i : 16 * (i + 1), :] = s
    sc = jnp.where(visible, score[...] * scale, -1e30)
    q = qs[...]
    f0 = jnp.sum(q * kx[0], -1, keepdims=True) * scale
    f1 = jnp.sum(q * kx[1], -1, keepdims=True) * scale
    f1 = jnp.where(tokstep > 0.5, f1, -1e30)
    top = jnp.maximum(jnp.max(sc, -1, keepdims=True), jnp.maximum(f0, f1))
    ex = jnp.exp(sc - top)
    e0 = jnp.exp(f0 - top)
    e1 = jnp.exp(f1 - top)
    den = jnp.sum(ex, -1, keepdims=True) + (e0 + e1)
    prob[...] = (ex / den).astype(BF16)
    p0 = (e0 / den).astype(BF16).astype(F32)
    p1 = (e1 / den).astype(BF16).astype(F32)
    att[...] = p0 * vx[0] + p1 * vx[1]
    ld_v.wait()
    for i in range(6):
        rows = slice(16 * i, 16 * (i + 1))
        p = prob[rows, :]
        s = dot(p, kvc[1, 4 * i])
        for b in range(1, 4):
            s = jnp.where(which == b, dot(p, kvc[1, 4 * i + b]), s)
        att[rows, :] = att[rows, :] + s
    for t in range(2):
        for g in range(2):
            att2[t, :, 128 * g : 128 * (g + 1)] = att[pl.ds(2 * t + g, ROWS, stride=4), :]
    attended = jnp.concatenate([att2[core], att2[other]], 0).astype(BF16)

    lot = jnp.concatenate([rmat[1, 0:64, :], rmat[1, 64:128, :]], 1)
    y = dot(attended, lot, NT)
    y = jnp.concatenate([y, jnp.zeros((2 * ROWS, 128 - RANK), F32)], 1)
    ybuf[...] = y[0:ROWS]
    ysend[0] = y[ROWS:].astype(BF16)
    ycopy = pltpu.make_async_remote_copy(
        ysend.at[0], yrecv, ysend_sem, yrecv_sem, device_id={"tensor": sib}, device_id_type=MESH)
    ycopy.start()

    def bcopy(n):
        return pltpu.make_async_remote_copy(
            bsend.at[n], brecv.at[n], bsend_sem.at[n], brecv_sem.at[n],
            device_id={"tensor": sib}, device_id_type=MESH)

    def ccopy(n):
        to = (chip + 1 + n) % CHIPS
        return pltpu.make_async_remote_copy(
            csend.at[n], crecv.at[chip], csend_sem.at[n], crecv_sem.at[chip],
            device_id={"tensor": 2 * to + core}, device_id_type=MESH)

    def y2copy(n):
        to = (chip + 1 + n) % CHIPS
        return pltpu.make_async_remote_copy(
            ysend.at[1], yall.at[chip], y2send_sem.at[n], y2recv_sem.at[chip],
            device_id={"tensor": 2 * to + core}, device_id_type=MESH)

    ld_wo.wait()
    for n in range(CHIPS):
        to = (chip + 1 + n) % CHIPS
        part = dot(attended, wo[:, pl.ds(pl.multiple_of(to * BLOCK, 128), BLOCK)])
        keep[n] = part[0:ROWS]
        bsend[n] = part[ROWS:].astype(BF16)
        bcopy(n).start()

    ycopy.wait_recv()
    ymine = ybuf[...] + yrecv[...].astype(F32)
    ysend[1] = ymine.astype(BF16)
    for n in range(CHIPS - 1):
        y2copy(n).start()
    for n in range(CHIPS - 1):
        bcopy(n).wait_recv()
        csend[n] = (keep[n] + brecv[n].astype(F32)).astype(BF16)
        ccopy(n).start()
    bcopy(CHIPS - 1).wait_recv()
    total = keep[CHIPS - 1] + brecv[CHIPS - 1].astype(F32)
    here = pl.ds(pl.multiple_of(chip * BLOCK, 128), BLOCK)
    total = total + tok[core, :, here].astype(F32)
    for n in range(CHIPS - 1):
        src = (chip + 1 + n) % CHIPS
        pltpu.make_async_copy(yall.at[src], yall.at[src], y2recv_sem.at[src]).wait()
        ymine = ymine + yall[src].astype(F32)
    ro = jnp.concatenate(
        [rmat[1, 128:192, :], rmat[1, 192:256, :], rmat[2, 0:64, :], rmat[2, 64:128, :],
         rmat[2, 128:192, :]], 1)
    total = total + 0.5 * dot(ymine[:, 0:RANK].astype(BF16), ro)
    for n in range(CHIPS - 1):
        src = (chip + 1 + n) % CHIPS
        pltpu.make_async_copy(crecv.at[src], crecv.at[src], crecv_sem.at[src]).wait()
        total = total + crecv[src].astype(F32)
    hid[core, :, here] = total.astype(BF16)

    def block(k, c):
        return hid.at[k, :, pl.ds(pl.multiple_of(c * BLOCK, 128), BLOCK)]

    def gcopy(n):
        to = (chip + 1 + n) % CHIPS
        return pltpu.make_async_remote_copy(
            block(core, chip), block(core, chip), gsend_sem.at[n], grecv_sem.at[chip],
            device_id={"tensor": 2 * to + core}, device_id_type=MESH)

    def fcopy(c):
        return pltpu.make_async_remote_copy(
            block(core, c), block(core, c), fsend_sem.at[c], frecv_sem.at[c],
            device_id={"tensor": sib}, device_id_type=MESH)

    for n in range(CHIPS - 1):
        gcopy(n).start()
    fcopy(chip).start()
    for n in range(CHIPS - 1):
        src = (chip + 1 + n) % CHIPS
        pltpu.make_async_copy(block(core, src), block(core, src), grecv_sem.at[src]).wait()
        fcopy(src).start()
    for n in range(CHIPS):
        c = (chip + n) % CHIPS
        pltpu.make_async_copy(block(other, c), block(other, c), frecv_sem.at[c]).wait()
    hid_out[...] = hid[...]

    @pl.when(active)
    def _():
        def done_l(d, _):
            lcopy(d).wait_send()
            return 0

        lax.fori_loop(1, DP, done_l, 0)

        def done_z(d, _):
            zcopy(d, (tp + d) % TP, slab, tp).wait_send()
            return 0

        lax.fori_loop(1, TP, done_z, 0)

    def done_p(d, _):
        pcopy(d).wait_send()
        return 0

    lax.fori_loop(1, DP, done_p, 0)
    ycopy.wait_send()
    for n in range(CHIPS):
        bcopy(n).wait_send()
        fcopy(n).wait_send()
    for n in range(CHIPS - 1):
        y2copy(n).wait_send()
        ccopy(n).wait_send()
        gcopy(n).wait_send()


def close_kernel(hid_ref, gain, kv_ref, hid_out, mlp_out, kv_out):
    kv_out[...] = kv_ref[...]
    sq = jnp.zeros((2, ROWS, 1), F32)
    for i in range(8):
        cols = slice(i * 640, (i + 1) * 640)
        v = hid_ref[:, :, cols]
        hid_out[:, :, cols] = v
        v = v.astype(F32)
        sq = sq + jnp.sum(v * v, -1, keepdims=True)
    rs = lax.rsqrt(sq * (1.0 / WIDTH) + 1e-06)
    for i in range(8):
        cols = slice(i * 640, (i + 1) * 640)
        v = hid_ref[:, :, cols].astype(F32) * rs * gain[:, cols][None]
        mlp_out[:, :, cols] = v.astype(BF16)


def shards(
    tokens_in, attn_gain, post_gain, w_query, key_weight_base, value_weight_base, w_out, left_qkv,
    right_query, right_key_value, left_out, right_out, kv_cache, lengths, starts,
):
    any_spec = pl.BlockSpec(memory_space=pl.ANY)
    vmem = pl.BlockSpec(memory_space=pltpu.VMEM)
    dma = pltpu.SemaphoreType.DMA
    scratch = [
        pltpu.VMEM((2, ROWS, WIDTH), BF16),
        pltpu.VMEM((1, WIDTH), F32),
        pltpu.VMEM((WIDTH, 512), BF16),
        pltpu.VMEM((256, WIDTH), BF16),
        pltpu.VMEM((2, ROWS, SLOTS, HEAD), BF16),
        pltpu.VMEM((1, ROWS), jnp.int32),
        pltpu.VMEM((1, ROWS), jnp.int32),
        pltpu.VMEM((LPAD, RANK), F32),
        pltpu.VMEM((4, 256), F32),
        pltpu.VMEM((2, 4, 128), F32),
        pltpu.VMEM((256, 4), F32),
        pltpu.VMEM((4, BLOCK), F32),
        pltpu.VMEM((16, LPAD), BF16),
        pltpu.VMEM((DP, 16, LPAD), BF16),
        pltpu.VMEM((48, 128), BF16),
        pltpu.VMEM((DP, 48, 128), BF16),
        pltpu.VMEM((12, 16, 128), BF16),
        pltpu.VMEM((3, 256, 128), BF16),
        pltpu.VMEM((2 * ROWS, WIDTH), BF16),
        pltpu.VMEM((2 * ROWS, 512), F32),
        pltpu.VMEM((4 * ROWS, HEAD), F32),
        pltpu.VMEM((2, 4 * ROWS, HEAD), F32),
        pltpu.VMEM((2, 4 * ROWS, HEAD), F32),
        pltpu.VMEM((4 * ROWS, SLOTS), F32),
        pltpu.VMEM((4 * ROWS, SLOTS), BF16),
        pltpu.VMEM((4 * ROWS, HEAD), F32),
        pltpu.VMEM((2, ROWS, 256), F32),
        pltpu.VMEM((ROWS, 128), F32),
        pltpu.VMEM((2, ROWS, 128), BF16),
        pltpu.VMEM((ROWS, 128), BF16),
        pltpu.VMEM((CHIPS, ROWS, 128), BF16),
        pltpu.VMEM((CHIPS, ROWS, BLOCK), F32),
        pltpu.VMEM((CHIPS, ROWS, BLOCK), BF16),
        pltpu.VMEM((CHIPS, ROWS, BLOCK), BF16),
        pltpu.VMEM((CHIPS, ROWS, BLOCK), BF16),
        pltpu.VMEM((CHIPS, ROWS, BLOCK), BF16),
        pltpu.VMEM((2, ROWS, WIDTH), BF16),
        dma((24,)),
        dma((DP,)), dma((DP,)), dma((DP,)), dma((DP,)), dma((TP,)), dma((12,)),
        dma, dma, dma((CHIPS,)), dma((CHIPS,)),
        dma((CHIPS,)), dma((CHIPS,)), dma((CHIPS,)), dma((CHIPS,)),
        dma((CHIPS,)), dma((CHIPS,)), dma((CHIPS,)), dma((CHIPS,)),
    ]
    hid, new_kv = pl.pallas_call(
        main_kernel,
        out_shape=(
            jax.ShapeDtypeStruct((2, ROWS, WIDTH), BF16),
            jax.ShapeDtypeStruct((2, 2, ROWS, HEAD), BF16),
        ),
        in_specs=[any_spec] * 14,
        out_specs=(vmem, vmem),
        scratch_shapes=scratch,
        compiler_params=pltpu.CompilerParams(
            collective_id=0, has_side_effects=True, vmem_limit_bytes=40 * 1024 * 1024),
    )(
        tokens_in, attn_gain.reshape(1, WIDTH), w_query, key_weight_base, value_weight_base, w_out,
        left_qkv, right_query, right_key_value, left_out, right_out, kv_cache,
        lengths.reshape(1, ROWS), starts.reshape(1, ROWS),
    )
    return pl.pallas_call(
        close_kernel,
        out_shape=(
            jax.ShapeDtypeStruct((2, ROWS, WIDTH), BF16),
            jax.ShapeDtypeStruct((2, ROWS, WIDTH), BF16),
            jax.ShapeDtypeStruct((2, 2, ROWS, HEAD), BF16),
        ),
        in_specs=[vmem] * 3,
        out_specs=(vmem, vmem, vmem),
    )(hid, post_gain.reshape(1, WIDTH), new_kv)


def solution(mesh):
    in_specs = (
        P(None, "dp", None),
        P(),
        P(),
        P(None, "tensor"),
        P(None, "tensor"),
        P(None, "tensor"),
        P("tensor", None),
        P(None, "dp", None),
        P("dp", "tensor"),
        P(None, "dp", "tensor"),
        P("tensor", "dp"),
        P("dp", None),
        P(None, "dp", "tensor", None, None),
        P("dp"),
        P("dp"),
    )
    out_specs = (P(None, "dp", None), P(None, "dp", None), P(None, None, "dp", "tensor"))
    return jax.shard_map(shards, mesh=mesh, in_specs=in_specs, out_specs=out_specs, check_vma=False)
```

time: 376 us -> 63.4 us (0.17)
  waiting for transfers between devices: 194 us -> 0 us
  blocking collectives: 110 us -> 0 us
  Pallas kernels: 0 us -> 45.2 us
  matrix products: 24.8 us -> 0 us
  between operations: 14.1 us -> 0.68 us
  other arithmetic: 6.54 us -> 0 us
  local copies, waits for them, and re-layouts: 22.4 us -> 16.9 us
    psum x1 -> x0, waiting for transfers between devices: 133 us -> none  [shards(): summed = lax.psum(partial_value, 'tensor')]
    all_gather x3 -> x0, blocking collectives: 110 us -> none  [the longest x1 41.1 us: shards(): lax.all_gather(right_query, 'dp', axis=0, tiled=True)]
    all_gather x2 -> x0, waiting for transfers between devices: 60.8 us -> none  [the longest x1 60.8 us: shards(): piece = lax.all_gather(left_qkv, 'dp', axis=1, tiled=True)]
    pallas_call x0 -> x2, Pallas kernels: none -> 45.2 us  [the longest x1 43.1 us: shards(): pl.pallas_call(main_kernel, out_shape=(jax.ShapeDtypeStruct((2, ROWS, WID...]
    dot_general x13 -> x0, matrix products: 24.8 us -> none  [the longest x3 9.09 us: shards(): jnp.dot(piece[index_num], right_part, precision=lax.Precision.HIGHEST)]
    slice x3 -> x0, local copies, waits for them, and re-layouts: 16.7 us -> none  [the longest x1 16.7 us: shards(): piece[index_num]]
    unnamed x29 -> x30, local copies, waits for them, and re-layouts: 5.65 us -> 16.9 us
  transfers between devices with their start and end apart: 3 -> 0, of which waited for: 2 -> 0; matrix products, arithmetic and copies ran while one was open for 4% -> 0% of each run, Pallas kernels for 0% -> 0%
where the time goes in v1:
time: 63.4 us; the launch traced here: 62.8 us
  Pallas kernels  45.2 us (71%)
  local copies, waits for them, and re-layouts  16.9 us (27%)
  between operations  0.68 us (1%)
    pallas_call x1, Pallas kernels, shards(): pl.pallas_call(main_kernel, out_shape=(jax.ShapeDtypeStruct((2, ROWS, WID...  43.1 us
    unnamed x30, local copies, waits for them, and re-layouts  16.9 us
    pallas_call x1, Pallas kernels, shards(): pl.pallas_call(close_kernel, out_shape=(jax.ShapeDtypeStruct((2, ROWS, WI...  2.14 us

profile of v1, /device:TPU:1, one launch (start us, length us, event | category | flops | bytes accessed | tf_op | source)
XLA Modules:
  0.0 62.8 jit_solution(6732710195413057468)
XLA Ops:
  0.6 0.8 %copy.19.lo_in = f32[256,4]{1,0:T(8,128)S(1)} copy(f32[256,4]{0,1:T(4,128)} %param.25) | data formatting | bytes 8192 | tf_op args[10]
  1.5 1.2 %copy.18.lqkv_in = f32[3,320,64]{2,1,0:T(8,128)S(1)} copy(f32[3,320,64]{1,2,0:T(8,128)} %param.22) | data formatting | bytes 491520 | tf_op args[7]
  2.6 0.0 copy-start
  2.6 2.1 %copy-done = bf16[2,24,1,320,128]{4,3,2,1,0:T(8,128)(2,1)S(1)} copy-done((bf16[2,24,1,320,128]{4,3,2,1,0:T(8,128)(2,1)S(1)}, bf16[2,24,1,320,128]{4,3,2,1,0:T(8,128)(2,1)}, u32[]{:S(2)}) %copy-start) | copy-done | bytes 3932184
  4.7 0.0 copy-start.1
  4.7 1.7 %copy-done.1 = bf16[5120,256]{1,0:T(8,128)(2,1)S(1)} copy-done((bf16[5120,256]{1,0:T(8,128)(2,1)S(1)}, bf16[5120,256]{1,0:T(8,128)(2,1)}, u32[]{:S(2)}) %copy-start.1) | copy-done | bytes 2621464
  6.5 0.0 copy-start.2
  6.5 1.7 %copy-done.2 = bf16[256,5120]{1,0:T(8,128)(2,1)S(1)} copy-done((bf16[256,5120]{1,0:T(8,128)(2,1)S(1)}, bf16[256,5120]{1,0:T(8,128)(2,1)}, u32[]{:S(2)}) %copy-start.2) | copy-done | bytes 2621464
  8.2 0.0 copy-start.3
  8.2 1.3 %copy-done.3 = bf16[5120,128]{1,0:T(8,128)(2,1)S(1)} copy-done((bf16[5120,128]{1,0:T(8,128)(2,1)S(1)}, bf16[5120,128]{1,0:T(8,128)(2,1)}, u32[]{:S(2)}) %copy-start.3) | copy-done | bytes 1310744
  9.5 0.0 copy-start.4
  9.5 1.3 %copy-done.4 = bf16[5120,128]{1,0:T(8,128)(2,1)S(1)} copy-done((bf16[5120,128]{1,0:T(8,128)(2,1)S(1)}, bf16[5120,128]{1,0:T(8,128)(2,1)}, u32[]{:S(2)}) %copy-start.4) | copy-done | bytes 1310744
  10.9 1.0 %copy-done.5 = bf16[2,24,5120]{2,1,0:T(8,128)(2,1)S(1)} copy-done((bf16[2,24,5120]{2,1,0:T(8,128)(2,1)S(1)}, bf16[2,24,5120]{2,1,0:T(8,128)(2,1)}, u32[]{:S(2)}) %copy-start.5) | copy-done | bytes 491544
  11.9 0.9 %copy-done.7 = f32[4,5120]{1,0:T(4,128)S(1)} copy-done((f32[4,5120]{1,0:T(4,128)S(1)}, f32[4,5120]{1,0:T(4,128)}, u32[]{:S(2)}) %copy-start.7) | copy-done | bytes 81944
  12.8 0.7 %copy-done.9 = f32[5120]{0:T(1024)S(1)} copy-done((f32[5120]{0:T(1024)S(1)}, f32[5120]{0:T(1024)}, u32[]{:S(2)}) %copy-start.9) | copy-done | bytes 20504
  13.5 0.7 %copy-done.10 = f32[4,256]{1,0:T(4,128)S(1)} copy-done((f32[4,256]{1,0:T(4,128)S(1)}, f32[4,256]{1,0:T(4,128)}, u32[]{:S(2)}) %copy-start.10) | copy-done | bytes 4120
  14.2 0.7 %copy-done.11 = f32[2,4,128]{2,1,0:T(4,128)S(1)} copy-done((f32[2,4,128]{2,1,0:T(4,128)S(1)}, f32[2,4,128]{2,1,0:T(4,128)}, u32[]{:S(2)}) %copy-start.11) | copy-done | bytes 4120
  14.9 0.7 %copy-done.12 = s32[24]{0:T(128)S(1)} copy-done((s32[24]{0:T(128)S(1)}, s32[24]{0:T(128)}, u32[]{:S(2)}) %copy-start.12) | copy-done | bytes 120
  15.5 0.7 %copy-done.13 = s32[24]{0:T(128)S(1)} copy-done((s32[24]{0:T(128)S(1)}, s32[24]{0:T(128)}, u32[]{:S(2)}) %copy-start.13) | copy-done | bytes 120
  16.2 43.1 %shard_map.166 = (bf16[2,24,5120]{2,1,0:T(8,128)(2,1)S(1)}, bf16[2,2,24,128]{3,2,1,0:T(8,128)(2,1)S(1)}) custom-call(bf16[2,24,5120]{2,1,0:T(8,128)(2,1)S(1)} %copy-done.5, f32[1,5120]{1,0:T(1,128)S(1)} %bitcast.4, bf16[5120,256]{1,0:T(8,128)(2,1)S(1)} %copy-done.1, bf16[5120,128]{1,0:T(8,128)(2,1)S(1)} %copy-done.3, bf16[5120,128]{1,0:T(8,128)(2,1)S(1)} %copy-done.4, ...), custom_call_target="tpu_custom_call" | custom-call | tf_op jit(solution)/shard_map/pallas_call | solution.py:489
  59.3 0.0 copy-start.6
  59.3 0.8 %copy-done.6 = bf16[2,24,5120]{2,1,0:T(8,128)(2,1)} copy-done((bf16[2,24,5120]{2,1,0:T(8,128)(2,1)}, bf16[2,24,5120]{2,1,0:T(8,128)(2,1)S(1)}, u32[]{:S(2)}) %copy-start.6) | copy-done | bytes 491544
  60.1 0.6 copy-done.8
  60.7 2.1 %shard_map.167 = (bf16[2,24,5120]{2,1,0:T(8,128)(2,1)}, bf16[2,24,5120]{2,1,0:T(8,128)(2,1)}, bf16[2,2,24,128]{3,2,1,0:T(8,128)(2,1)}) custom-call(bf16[2,24,5120]{2,1,0:T(8,128)(2,1)} %copy-done.6, f32[1,5120]{1,0:T(1,128)} %bitcast.7, bf16[2,2,24,128]{3,2,1,0:T(8,128)(2,1)} %copy-done.8), custom_call_target="tpu_custom_call" | custom-call | tf_op jit(solution)/shard_map/pallas_call | solution.py:505
  (8 shorter events, 0.0 us)
Async XLA Ops:
  2.6 2.1 %copy-start = (bf16[2,24,1,320,128]{4,3,2,1,0:T(8,128)(2,1)S(1)}, bf16[2,24,1,320,128]{4,3,2,1,0:T(8,128)(2,1)}, u32[]{:S(2)}) copy-start(bf16[2,24,1,320,128]{4,3,2,1,0:T(8,128)(2,1)} %kv_in.1) | copy-start | bytes 11796484
  4.7 1.7 %copy-start.1 = (bf16[5120,256]{1,0:T(8,128)(2,1)S(1)}, bf16[5120,256]{1,0:T(8,128)(2,1)}, u32[]{:S(2)}) copy-start(bf16[5120,256]{1,0:T(8,128)(2,1)} %wq_in.1) | copy-start | bytes 7864324
  6.5 1.7 %copy-start.2 = (bf16[256,5120]{1,0:T(8,128)(2,1)S(1)}, bf16[256,5120]{1,0:T(8,128)(2,1)}, u32[]{:S(2)}) copy-start(bf16[256,5120]{1,0:T(8,128)(2,1)} %wo_in.1) | copy-start | bytes 7864324
  8.2 1.3 %copy-start.3 = (bf16[5120,128]{1,0:T(8,128)(2,1)S(1)}, bf16[5120,128]{1,0:T(8,128)(2,1)}, u32[]{:S(2)}) copy-start(bf16[5120,128]{1,0:T(8,128)(2,1)} %wk_in.1) | copy-start | bytes 3932164
  9.5 1.3 %copy-start.4 = (bf16[5120,128]{1,0:T(8,128)(2,1)S(1)}, bf16[5120,128]{1,0:T(8,128)(2,1)}, u32[]{:S(2)}) copy-start(bf16[5120,128]{1,0:T(8,128)(2,1)} %wv_in.1) | copy-start | bytes 3932164
  10.9 1.0 %copy-start.5 = (bf16[2,24,5120]{2,1,0:T(8,128)(2,1)S(1)}, bf16[2,24,5120]{2,1,0:T(8,128)(2,1)}, u32[]{:S(2)}) copy-start(bf16[2,24,5120]{2,1,0:T(8,128)(2,1)} %tok_in.1) | copy-start | bytes 1474564
  11.9 0.9 %copy-start.7 = (f32[4,5120]{1,0:T(4,128)S(1)}, f32[4,5120]{1,0:T(4,128)}, u32[]{:S(2)}) copy-start(f32[4,5120]{1,0:T(4,128)} %ro_in.1) | copy-start | bytes 245764
  12.8 0.7 %copy-start.9 = (f32[5120]{0:T(1024)S(1)}, f32[5120]{0:T(1024)}, u32[]{:S(2)}) copy-start(f32[5120]{0:T(1024)} %param.16) | copy-start | bytes 61444
  13.5 0.7 %copy-start.10 = (f32[4,256]{1,0:T(4,128)S(1)}, f32[4,256]{1,0:T(4,128)}, u32[]{:S(2)}) copy-start(f32[4,256]{1,0:T(4,128)} %rq_in.1) | copy-start | bytes 12292
  14.2 0.7 %copy-start.11 = (f32[2,4,128]{2,1,0:T(4,128)S(1)}, f32[2,4,128]{2,1,0:T(4,128)}, u32[]{:S(2)}) copy-start(f32[2,4,128]{2,1,0:T(4,128)} %rkv_in.1) | copy-start | bytes 12292
  14.9 0.7 %copy-start.12 = (s32[24]{0:T(128)S(1)}, s32[24]{0:T(128)}, u32[]{:S(2)}) copy-start(s32[24]{0:T(128)} %param.28) | copy-start | bytes 292
  15.5 0.7 %copy-start.13 = (s32[24]{0:T(128)S(1)}, s32[24]{0:T(128)}, u32[]{:S(2)}) copy-start(s32[24]{0:T(128)} %param.29) | copy-start | bytes 292
  59.3 0.8 %copy-start.6 = (bf16[2,24,5120]{2,1,0:T(8,128)(2,1)}, bf16[2,24,5120]{2,1,0:T(8,128)(2,1)S(1)}, u32[]{:S(2)}) copy-start(bf16[2,24,5120]{2,1,0:T(8,128)(2,1)S(1)} %get-tuple-element.5.hid_ref) | copy-start | bytes 1474564
  60.1 0.6 copy-start.8

commit v2 on v1

v2 whole, which is shorter than its diff:
```python
import math

import jax
import jax.numpy as jnp
from jax import lax
from jax.experimental import pallas as pl
from jax.experimental.pallas import tpu as pltpu
from jax.sharding import PartitionSpec as P

MESH = pl.DeviceIdType.MESH
BF16 = jnp.bfloat16
F32 = jnp.float32

WIDTH = 5120
HEAD = 128
SLOTS = 320
WINDOW = 256
RANK = 64
ROWS = 24
DP = 16
TP = 16
CHIPS = 8
XS = 4
HALF = WIDTH // 2
BLOCK = HALF // XS
LROWS = WIDTH // DP
LPAD = 384
NT = (((1,), (1,)), ((), ()))
TN = (((0,), (0,)), ((), ()))
NN = (((1,), (0,)), ((), ()))


def dot(a, b, dims=NN):
    return lax.dot_general(a, b, dims, preferred_element_type=F32)


def iota(shape, axis):
    return lax.broadcasted_iota(jnp.int32, shape, axis)


def one_hot(cond):
    return jnp.where(cond, 1.0, 0.0).astype(BF16)


def main_kernel(
    tok_in, gain_in, pgain_in, wq_in, wk_in, wv_in, wo_in, lqkv_in, rq_in, rkv_in, lo_in, ro_in,
    kv_in, len_in, start_in,
    hid_out, mlp_out, kv_out,
    tok, gain, pgain, w, wo, kvc, lens, starts,
    lbuf, rq, rkv, lob, rob,
    lsend, lgat, packa, packb, pagat, pbgat, zgat, rmat, losib,
    normed, proj, qs, kx, vx, score, prob, att, attboth, ysend, yall, csend, crecv, hid,
    loc, lsend_sem, lrecv_sem, asend_sem, arecv_sem, psend_sem, precv_sem, zsend_sem, zrecv_sem,
    sib_send, sib_recv, ysend_sem, yrecv_sem, csend_sem, crecv_sem,
    gsend_sem, grecv_sem, fsend_sem, frecv_sem,
):
    dp = lax.axis_index("dp")
    tp = lax.axis_index("tensor")
    chip = tp // 2
    core = tp % 2
    zlo = chip // XS
    xpos = chip % XS
    sib = tp + 1 - 2 * core
    other = 1 - core
    pend = {}

    def finish():
        for wait in pend.values():
            wait()

    def load(name, src, dst):
        c = pltpu.make_async_copy(src, dst, loc.at[len(pend)])
        c.start()
        pend[name] = c.wait

    def ready(*names):
        for name in names:
            pend.pop(name)()

    active = jnp.logical_or(tp < 8, core == 0)
    slab = jnp.where(tp < 8, tp, tp // 2 + 4)
    mine = core * HALF + xpos * BLOCK
    load("l", lqkv_in.at[slab // 4, pl.ds(pl.multiple_of(16 * (slab % 4), 16), 16)], lbuf)
    load("rq", rq_in, rq)
    load("rkv", rkv_in, rkv)
    load("lo", lo_in, lob)
    load("ro", ro_in.at[:, pl.ds(pl.multiple_of(mine, 128), BLOCK)], rob)
    load("tok", tok_in, tok)
    load("gain", gain_in, gain)
    load("len", len_in, lens)
    load("start", start_in, starts)
    step = WIDTH // 4
    for i in range(4):
        rs = pl.ds(i * step, step)
        load(("wq", i), wq_in.at[rs], w.at[rs, 0:256])
        load(("wk", i), wk_in.at[rs], w.at[rs, 256:384])
        load(("wv", i), wv_in.at[rs], w.at[rs, 384:512])
    load("k", kv_in.at[0, :, 0], kvc.at[0])
    load("v", kv_in.at[1, :, 0], kvc.at[1])
    load("wo", wo_in.at[:, pl.ds(pl.multiple_of(core * HALF, 128), HALF)], wo.at[0:256])
    load("pgain", pgain_in, pgain)

    barrier = pltpu.get_barrier_semaphore()

    def greet(d, _):
        pl.semaphore_signal(
            barrier, inc=1, device_id={"dp": (dp + d) % DP}, device_id_type=MESH)
        pl.semaphore_signal(
            barrier, inc=1, device_id={"tensor": (tp + d) % TP}, device_id_type=MESH)
        return 0

    lax.fori_loop(1, DP, greet, 0)

    ready("l")
    rank_rows = jnp.concatenate([lbuf[...], jnp.zeros((16, LPAD - LROWS), F32)], 1)
    rank_rows = jnp.where(dp % 2 == 1, pltpu.roll(rank_rows, LPAD - LROWS, 1), rank_rows)
    lsend[...] = rank_rows.astype(BF16)
    lgat[dp] = lsend[...]

    pl.semaphore_wait(barrier, 2 * (DP - 1))

    def gather(src, dst, send, recv, name):
        def copy(d):
            to = (dp + d) % DP
            return pltpu.make_async_remote_copy(
                src, dst.at[dp], send.at[d], recv.at[dp],
                device_id={"dp": to}, device_id_type=MESH)

        def go(d, _):
            copy(d).start()
            return 0

        def sent(d, _):
            copy(d).wait_send()
            return 0

        def got(d, _):
            who = (dp + d) % DP
            pltpu.make_async_copy(dst.at[who], dst.at[who], recv.at[who]).wait()
            return 0

        lax.fori_loop(1, DP, go, 0)
        pend[name, "sent"] = lambda: lax.fori_loop(1, DP, sent, 0)
        pend[name] = lambda: lax.fori_loop(1, DP, got, 0)

    def when_active(f):
        @pl.when(active)
        def _():
            f()

    @pl.when(active)
    def _():
        gather(lsend, lgat, lsend_sem, lrecv_sem, "L")

    lsent, lgot = pend.pop(("L", "sent")), pend.pop("L")
    pend["L", "sent"] = lambda: when_active(lsent)
    pend["L"] = lambda: when_active(lgot)

    ready("rq", "rkv")
    tiles = [rq[:, 0:128], rq[:, 128:256], rkv[0], rkv[1]]
    packa[...] = jnp.concatenate(tiles, 0).astype(BF16)
    pagat[dp] = packa[...]
    gather(packa, pagat, asend_sem, arecv_sem, "A")
    ready("lo", "ro")
    tiles = [lob[:, 0:128], lob[:, 128:256]]
    tiles += [rob[:, 128 * i : 128 * (i + 1)] for i in range(5)]
    tiles += [jnp.zeros((4, 128), F32)]
    packb[...] = jnp.concatenate(tiles, 0).astype(BF16)
    pbgat[dp] = packb[...]
    gather(packb, pbgat, psend_sem, precv_sem, "B")

    def to_sib(src, dst, k, name):
        c = pltpu.make_async_remote_copy(
            src, dst, sib_send.at[k], sib_recv.at[k],
            device_id={"tensor": sib}, device_id_type=MESH)
        c.start()
        pend[name, "sent"] = c.wait_send
        pend[name] = c.wait_recv

    to_sib(wo_in.at[:, pl.ds(pl.multiple_of(other * HALF, 128), HALF)], wo.at[256:512], 0, "wosib")


    ready("tok", "gain")
    sq = jnp.zeros((2, ROWS, 1), F32)
    for i in range(8):
        v = tok[:, :, i * 640 : (i + 1) * 640].astype(F32)
        sq = sq + jnp.sum(v * v, -1, keepdims=True)
    rs = lax.rsqrt(sq * (1.0 / WIDTH) + 1e-06)
    for i in range(8):
        cols = slice(i * 640, (i + 1) * 640)
        v = tok[:, :, cols].astype(F32) * rs * gain[:, cols][None]
        normed[:, cols] = v.reshape(2 * ROWS, 640).astype(BF16)

    acc = None
    for i in range(2):
        ready(("wq", i), ("wk", i), ("wv", i))
        part = dot(normed[:, i * step : (i + 1) * step], w[i * step : (i + 1) * step, :])
        acc = part if acc is None else acc + part
    proj[...] = acc

    ready("L")

    def zcopy(d):
        return pltpu.make_async_remote_copy(
            zgat.at[slab], zgat.at[slab], zsend_sem.at[d], zrecv_sem.at[slab],
            device_id={"tensor": (tp + d) % TP}, device_id_type=MESH)

    @pl.when(active)
    def _():
        parts = []
        for j in range(0, DP, 2):
            parts += [lgat[j, :, 0:256], lgat[j, :, 256:384] + lgat[j + 1, :, 0:128]]
            parts += [lgat[j + 1, :, 128:384]]
        z = dot(jnp.concatenate(parts, 1), normed[...], NT)
        z = jnp.concatenate([z, jnp.zeros((16, 128 - 2 * ROWS), F32)], 1)
        zgat[slab] = z.astype(BF16)

        def send_z(d, _):
            zcopy(d).start()
            return 0

        lax.fori_loop(1, TP, send_z, 0)

    def sent_z():
        def sent(d, _):
            zcopy(d).wait_send()
            return 0

        when_active(lambda: lax.fori_loop(1, TP, sent, 0))

    def got_z():
        def got(s, _):
            src = jnp.where(s < 8, s, 2 * s - 8)

            @pl.when(src != tp)
            def _():
                pltpu.make_async_copy(zgat.at[s], zgat.at[s], zrecv_sem.at[s]).wait()

            return 0

        lax.fori_loop(0, 12, got, 0)

    pend["Z", "sent"] = sent_z
    pend["Z"] = got_z
    acc = proj[...]
    for i in range(2, 4):
        ready(("wq", i), ("wk", i), ("wv", i))
        acc = acc + dot(normed[:, i * step : (i + 1) * step], w[i * step : (i + 1) * step, :])
    proj[...] = acc

    ready("len", "start")
    lenf = lens[...].astype(F32)
    stf = starts[...].astype(F32)

    def column(values, rows, owner):
        hit = owner(iota((rows, ROWS), 0)) == iota((rows, ROWS), 1)
        return jnp.sum(jnp.where(hit, values, 0.0), -1, keepdims=True)

    row = iota((2 * ROWS, 1), 0)
    pos = column(lenf, 2 * ROWS, lambda r: r % ROWS) + jnp.where(row >= ROWS, 1.0, 0.0)
    lane = iota((1, HEAD), 1)
    freq = jnp.exp((lane % 64).astype(F32) * (-2.0 * math.log(1000000.0) / HEAD))
    angle = pos * freq
    cos = jnp.cos(angle)
    sin = jnp.sin(angle) * jnp.where(lane < 64, -1.0, 1.0)

    def rope(v):
        return v * cos + pltpu.roll(v, 64, 1) * sin

    arow = iota((4 * ROWS, 1), 0)
    tokstep = jnp.where(arow % 4 >= 2, 1.0, 0.0)
    alen = column(lenf, 4 * ROWS, lambda r: r // 4)
    ast = column(stf, 4 * ROWS, lambda r: r // 4)
    slot = iota((4 * ROWS, SLOTS), 1).astype(F32) - ast
    slot = jnp.where(slot < 0, slot + float(SLOTS), slot)
    visible = jnp.logical_and(slot < alen, alen + tokstep - slot < float(WINDOW))

    ready("A")
    o = iota((256, 256), 0)
    perm = one_hot(iota((256, 256), 1) == ((o % 64) // 4) * 16 + 4 * (o // 64) + o % 4)
    rmat[0] = dot(perm, pagat[...].reshape(256, 128)).astype(BF16)

    ready("Z")
    cols = []
    for t, p in enumerate((0, 0, 1, 2)):
        z = zgat[4 * p : 4 * (p + 1)].reshape(RANK, 128)
        delta = dot(z, rmat[0, 64 * t : 64 * (t + 1), :], TN)[: 2 * ROWS]
        cols.append(proj[:, 128 * t : 128 * (t + 1)] + 0.5 * delta)
    rounded = [rope(cols[0]), rope(cols[1]), rope(cols[2]), cols[3]]
    rounded = [v.astype(BF16).astype(F32) for v in rounded]
    for t in range(2):
        rows = slice(t * ROWS, (t + 1) * ROWS)
        kv_out[t, 0] = rounded[2][rows].astype(BF16)
        kv_out[t, 1] = rounded[3][rows].astype(BF16)
        for g in range(2):
            qs[pl.ds(2 * t + g, ROWS, stride=4), :] = rounded[g][rows]
        for r in range(4):
            kx[t, pl.ds(r, ROWS, stride=4), :] = rounded[2][rows]
            vx[t, pl.ds(r, ROWS, stride=4), :] = rounded[3][rows]

    scale = 1.0 / math.sqrt(HEAD)
    ready("k")
    which = iota((16, 1), 0) // 4
    for i in range(6):
        q = qs[16 * i : 16 * (i + 1), :].astype(BF16)
        s = dot(q, kvc[0, 4 * i], NT)
        for b in range(1, 4):
            s = jnp.where(which == b, dot(q, kvc[0, 4 * i + b], NT), s)
        score[16 * i : 16 * (i + 1), :] = s
    sc = jnp.where(visible, score[...] * scale, -1e30)
    q = qs[...]
    f0 = jnp.sum(q * kx[0], -1, keepdims=True) * scale
    f1 = jnp.sum(q * kx[1], -1, keepdims=True) * scale
    f1 = jnp.where(tokstep > 0.5, f1, -1e30)
    top = jnp.maximum(jnp.max(sc, -1, keepdims=True), jnp.maximum(f0, f1))
    ex = jnp.exp(sc - top)
    e0 = jnp.exp(f0 - top)
    e1 = jnp.exp(f1 - top)
    den = jnp.sum(ex, -1, keepdims=True) + (e0 + e1)
    prob[...] = (ex / den).astype(BF16)
    p0 = (e0 / den).astype(BF16).astype(F32)
    p1 = (e1 / den).astype(BF16).astype(F32)
    att[...] = p0 * vx[0] + p1 * vx[1]
    ready("v")
    for i in range(6):
        rows = slice(16 * i, 16 * (i + 1))
        p = prob[rows, :]
        s = dot(p, kvc[1, 4 * i])
        for b in range(1, 4):
            s = jnp.where(which == b, dot(p, kvc[1, 4 * i + b]), s)
        att[rows, :] = att[rows, :] + s
    heads = []
    for g in range(2):
        heads.append(jnp.concatenate([att[pl.ds(2 * t + g, ROWS, stride=4), :] for t in range(2)], 0))
    attboth[0] = jnp.concatenate(heads, 1).astype(BF16)

    to_sib(attboth.at[0], attboth.at[1], 1, "att")
    ready("B")
    grp = pbgat[:, 0:16, :].reshape(256, 128)
    rmat[1] = dot(perm, grp).astype(BF16)
    losib[0] = rmat[1, 0:128, :]
    to_sib(losib.at[0], losib.at[1], 2, "losib")
    grp = pbgat[:, 16:32, :].reshape(256, 128)
    rmat[2] = dot(perm, grp).astype(BF16)

    def ccopy(c):
        return pltpu.make_async_remote_copy(
            csend.at[c], crecv.at[chip], csend_sem.at[c], crecv_sem.at[chip],
            device_id={"tensor": 2 * c + core}, device_id_type=MESH)

    def ycopy(c):
        return pltpu.make_async_remote_copy(
            ysend.at[c // XS], yall.at[chip], ysend_sem.at[c], yrecv_sem.at[chip],
            device_id={"tensor": 2 * c + core}, device_id_type=MESH)

    ready("wo", "wosib", "att")
    both = jnp.concatenate([attboth[0], attboth[1]], 1)
    total = None
    for n in (2, 1, 3, 0):
        x = (xpos + n) % XS
        part = dot(both, wo[:, pl.ds(pl.multiple_of(x * BLOCK, 128), BLOCK)])
        for t in range(2):
            csend[t * XS + x] = part[t * ROWS : (t + 1) * ROWS].astype(BF16)
            if n != 0:
                ccopy(t * XS + x).start()
        if n == 0:
            ccopy((1 - zlo) * XS + x).start()
            total = jnp.where(zlo == 0, part[0:ROWS], part[ROWS:])

    def peers(f):
        def body(n, _):
            f((chip + n) % CHIPS)
            return 0

        lax.fori_loop(1, CHIPS, body, 0)

    pend["C", "sent"] = lambda: peers(lambda c: ccopy(c).wait_send())

    ready("losib")
    lot = jnp.concatenate([losib[0, 0:64], losib[0, 64:128], losib[1, 0:64], losib[1, 64:128]], 1)
    y = dot(both, lot, NT)
    y = jnp.concatenate([y, jnp.zeros((2 * ROWS, 128 - RANK), F32)], 1)
    ysend[0] = y[0:ROWS].astype(BF16)
    ysend[1] = y[ROWS:].astype(BF16)
    peers(lambda c: ycopy(c).start())
    pend["Y", "sent"] = lambda: peers(lambda c: ycopy(c).wait_send())
    total = total + tok[zlo, :, pl.ds(pl.multiple_of(mine, 128), BLOCK)].astype(F32)
    ysum = jnp.where(zlo == 0, y[0:ROWS], y[ROWS:])
    for n in range(1, CHIPS):
        src = (chip + n) % CHIPS
        pltpu.make_async_copy(yall.at[src], yall.at[src], yrecv_sem.at[src]).wait()
        ysum = ysum + yall[src].astype(F32)
    ro = jnp.concatenate(
        [rmat[1, 128:192, :], rmat[1, 192:256, :], rmat[2, 0:64, :], rmat[2, 64:128, :],
         rmat[2, 128:192, :]], 1)
    total = total + 0.5 * dot(ysum[:, 0:RANK].astype(BF16), ro)
    for n in range(1, CHIPS):
        src = (chip + n) % CHIPS
        pltpu.make_async_copy(crecv.at[src], crecv.at[src], crecv_sem.at[src]).wait()
        total = total + crecv[src].astype(F32)
    hid[zlo, :, pl.ds(pl.multiple_of(mine, 128), BLOCK)] = total.astype(BF16)

    def block(k, c):
        return hid.at[c // XS, :, pl.ds(pl.multiple_of(k * HALF + (c % XS) * BLOCK, 128), BLOCK)]

    def gcopy(c):
        return pltpu.make_async_remote_copy(
            block(core, chip), block(core, chip), gsend_sem.at[c], grecv_sem.at[chip],
            device_id={"tensor": 2 * c + core}, device_id_type=MESH)

    def fcopy(c):
        return pltpu.make_async_remote_copy(
            block(core, c), block(core, c), fsend_sem.at[c], frecv_sem.at[c],
            device_id={"tensor": sib}, device_id_type=MESH)

    peers(lambda c: gcopy(c).start())
    pend["G", "sent"] = lambda: peers(lambda c: gcopy(c).wait_send())
    fcopy(chip).start()
    pend["F0", "sent"] = lambda: fcopy(chip).wait_send()
    pend["F", "sent"] = lambda: peers(lambda c: fcopy(c).wait_send())
    for n in range(1, CHIPS):
        src = (chip + n) % CHIPS
        pltpu.make_async_copy(block(core, src), block(core, src), grecv_sem.at[src]).wait()
        fcopy(src).start()
    for n in range(CHIPS):
        c = (chip + n) % CHIPS
        pltpu.make_async_copy(block(other, c), block(other, c), frecv_sem.at[c]).wait()

    ready("pgain")
    sq = jnp.zeros((2, ROWS, 1), F32)
    for i in range(8):
        cols = slice(i * 640, (i + 1) * 640)
        v = hid[:, :, cols]
        hid_out[:, :, cols] = v
        v = v.astype(F32)
        sq = sq + jnp.sum(v * v, -1, keepdims=True)
    rs = lax.rsqrt(sq * (1.0 / WIDTH) + 1e-06)
    for i in range(8):
        cols = slice(i * 640, (i + 1) * 640)
        v = hid[:, :, cols].astype(F32) * rs * pgain[:, cols][None]
        mlp_out[:, :, cols] = v.astype(BF16)

    finish()


def close_kernel(hid_ref, mlp_ref, kv_ref, hid_out, mlp_out, kv_out, sems):
    copies = []
    for k, (src, dst) in enumerate(((hid_ref, hid_out), (mlp_ref, mlp_out), (kv_ref, kv_out))):
        copies.append(pltpu.make_async_copy(src, dst, sems.at[k]))
    for c in copies:
        c.start()
    for c in copies:
        c.wait()


def shards(
    tokens_in, attn_gain, post_gain, w_query, key_weight_base, value_weight_base, w_out, left_qkv,
    right_query, right_key_value, left_out, right_out, kv_cache, lengths, starts,
):
    hbm = pl.BlockSpec(memory_space=pltpu.HBM)
    vmem = pl.BlockSpec(memory_space=pltpu.VMEM)
    dma = pltpu.SemaphoreType.DMA
    scratch = [
        pltpu.VMEM((2, ROWS, WIDTH), BF16),
        pltpu.VMEM((1, WIDTH), F32),
        pltpu.VMEM((1, WIDTH), F32),
        pltpu.VMEM((WIDTH, 512), BF16),
        pltpu.VMEM((512, HALF), BF16),
        pltpu.VMEM((2, ROWS, SLOTS, HEAD), BF16),
        pltpu.VMEM((1, ROWS), jnp.int32),
        pltpu.VMEM((1, ROWS), jnp.int32),
        pltpu.VMEM((16, LROWS), F32),
        pltpu.VMEM((4, 256), F32),
        pltpu.VMEM((2, 4, 128), F32),
        pltpu.VMEM((4, 256), F32),
        pltpu.VMEM((4, BLOCK), F32),
        pltpu.VMEM((16, LPAD), BF16),
        pltpu.VMEM((DP, 16, LPAD), BF16),
        pltpu.VMEM((16, 128), BF16),
        pltpu.VMEM((32, 128), BF16),
        pltpu.VMEM((DP, 16, 128), BF16),
        pltpu.VMEM((DP, 32, 128), BF16),
        pltpu.VMEM((12, 16, 128), BF16),
        pltpu.VMEM((3, 256, 128), BF16),
        pltpu.VMEM((2, 128, 128), BF16),
        pltpu.VMEM((2 * ROWS, WIDTH), BF16),
        pltpu.VMEM((2 * ROWS, 512), F32),
        pltpu.VMEM((4 * ROWS, HEAD), F32),
        pltpu.VMEM((2, 4 * ROWS, HEAD), F32),
        pltpu.VMEM((2, 4 * ROWS, HEAD), F32),
        pltpu.VMEM((4 * ROWS, SLOTS), F32),
        pltpu.VMEM((4 * ROWS, SLOTS), BF16),
        pltpu.VMEM((4 * ROWS, HEAD), F32),
        pltpu.VMEM((2, 2 * ROWS, 256), BF16),
        pltpu.VMEM((2, ROWS, 128), BF16),
        pltpu.VMEM((CHIPS, ROWS, 128), BF16),
        pltpu.VMEM((CHIPS, ROWS, BLOCK), BF16),
        pltpu.VMEM((CHIPS, ROWS, BLOCK), BF16),
        pltpu.VMEM((2, ROWS, WIDTH), BF16),
        dma((32,)),
        dma((DP,)), dma((DP,)), dma((DP,)), dma((DP,)), dma((DP,)), dma((DP,)),
        dma((TP,)), dma((12,)), dma((3,)), dma((3,)),
        dma((CHIPS,)), dma((CHIPS,)), dma((CHIPS,)), dma((CHIPS,)),
        dma((CHIPS,)), dma((CHIPS,)), dma((CHIPS,)), dma((CHIPS,)),
    ]
    shapes = (
        jax.ShapeDtypeStruct((2, ROWS, WIDTH), BF16),
        jax.ShapeDtypeStruct((2, ROWS, WIDTH), BF16),
        jax.ShapeDtypeStruct((2, 2, ROWS, HEAD), BF16),
    )
    args = (
        tokens_in, attn_gain.reshape(1, WIDTH), post_gain.reshape(1, WIDTH), w_query,
        key_weight_base, value_weight_base, w_out, left_qkv.swapaxes(1, 2), right_query,
        right_key_value, left_out.T, right_out, kv_cache, lengths.reshape(1, ROWS),
        starts.reshape(1, ROWS),
    )
    results = pl.pallas_call(
        main_kernel,
        out_shape=tuple(pltpu.VMEM(s.shape, s.dtype) for s in shapes),
        in_specs=[hbm] * len(args),
        out_specs=(vmem, vmem, vmem),
        scratch_shapes=scratch,
        compiler_params=pltpu.CompilerParams(
            collective_id=0, has_side_effects=True, vmem_limit_bytes=40 * 1024 * 1024),
    )(*[pltpu.with_memory_space_constraint(a, pltpu.HBM) for a in args])
    return pl.pallas_call(
        close_kernel,
        out_shape=shapes,
        in_specs=[vmem] * 3,
        out_specs=(hbm, hbm, hbm),
        scratch_shapes=[dma((3,))],
    )(*[pltpu.with_memory_space_constraint(a, pltpu.VMEM) for a in results])


def solution(mesh):
    in_specs = (
        P(None, "dp", None),
        P(),
        P(),
        P(None, "tensor"),
        P(None, "tensor"),
        P(None, "tensor"),
        P("tensor", None),
        P(None, "dp", None),
        P("dp", "tensor"),
        P(None, "dp", "tensor"),
        P("tensor", "dp"),
        P("dp", None),
        P(None, "dp", "tensor", None, None),
        P("dp"),
        P("dp"),
    )
    out_specs = (P(None, "dp", None), P(None, "dp", None), P(None, None, "dp", "tensor"))
    return jax.shard_map(shards, mesh=mesh, in_specs=in_specs, out_specs=out_specs, check_vma=False)
```

time: 63.4 us -> 43.8 us (0.69)
  local copies, waits for them, and re-layouts: 16.9 us -> 0 us
  Pallas kernels: 45.2 us -> 43.1 us
    unnamed x30 -> x0, local copies, waits for them, and re-layouts: 16.9 us -> none
    pallas_call x2, Pallas kernels: 45.2 us -> 43.1 us  [the longest x1 42.1 us: shards(): pl.pallas_call(main_kernel, out_shape=tuple((pltpu.VMEM(s.shape, s.dtype)...]
where the time goes in v2:
time: 43.8 us
  Pallas kernels  43.1 us (98%)
  between operations  0.64 us (1%)
    pallas_call x1, Pallas kernels, shards(): pl.pallas_call(main_kernel, out_shape=tuple((pltpu.VMEM(s.shape, s.dtype)...  42.1 us
    pallas_call x1, Pallas kernels, shards(): pl.pallas_call(close_kernel, out_shape=shapes, in_specs=[vmem] * 3, out_s...  0.97 us

profile of v2, /device:TPU:1, one launch (start us, length us, event | category | flops | bytes accessed | tf_op | source)
XLA Modules:
  0.0 43.8 jit_solution(18169894332637876514)
XLA Ops:
  0.6 42.1 %shard_map.166 = (bf16[2,24,5120]{2,1,0:T(8,128)(2,1)S(1)}, bf16[2,24,5120]{2,1,0:T(8,128)(2,1)S(1)}, bf16[2,2,24,128]{3,2,1,0:T(8,128)(2,1)S(1)}) custom-call(bf16[2,24,5120]{2,1,0:T(8,128)(2,1)} %tok_in.1, f32[1,5120]{1,0:T(1,128)} %bitcast.7, f32[1,5120]{1,0:T(1,128)} %bitcast.8, bf16[5120,256]{1,0:T(8,128)(2,1)} %wq_in.1, bf16[5120,128]{1,0:T(8,128)(2,1)} %wk_in.1, ...), custom_call_target="tpu_custom_call" | custom-call | tf_op jit(solution)/shard_map/pallas_call | solution.py:517
  42.8 1.0 %shard_map.167 = (bf16[2,24,5120]{2,1,0:T(8,128)(2,1)}, bf16[2,24,5120]{2,1,0:T(8,128)(2,1)}, bf16[2,2,24,128]{3,2,1,0:T(8,128)(2,1)}) custom-call(bf16[2,24,5120]{2,1,0:T(8,128)(2,1)S(1)} %get-tuple-element.6.hid_ref, bf16[2,24,5120]{2,1,0:T(8,128)(2,1)S(1)} %get-tuple-element.7.mlp_ref, bf16[2,2,24,128]{3,2,1,0:T(8,128)(2,1)S(1)} %get-tuple-element.8.kv_ref), custom_call_target="tpu_custom_call" | custom-call | tf_op jit(solution)/shard_map/pallas_call | solution.py:526

commit v3 on v2

v3 whole, which is shorter than its diff:
```python
import math

import jax
import jax.numpy as jnp
from jax import lax
from jax.experimental import pallas as pl
from jax.experimental.pallas import tpu as pltpu
from jax.sharding import PartitionSpec as P

MESH = pl.DeviceIdType.MESH
BF16 = jnp.bfloat16
F32 = jnp.float32

WIDTH = 5120
HEAD = 128
SLOTS = 320
WINDOW = 256
RANK = 64
ROWS = 24
DP = 16
TP = 16
CHIPS = 8
XS = 4
HALF = WIDTH // 2
BLOCK = HALF // XS
PARTS = ((0, 256), (256, 384))
LROWS = WIDTH // DP
LPAD = 384
NT = (((1,), (1,)), ((), ()))
TN = (((0,), (0,)), ((), ()))
NN = (((1,), (0,)), ((), ()))


def dot(a, b, dims=NN):
    return lax.dot_general(a, b, dims, preferred_element_type=F32)


def iota(shape, axis):
    return lax.broadcasted_iota(jnp.int32, shape, axis)


def one_hot(cond):
    return jnp.where(cond, 1.0, 0.0).astype(BF16)


def main_kernel(
    tok_in, gain_in, pgain_in, wq_in, wk_in, wv_in, wo_in, lqkv_in, rq_in, rkv_in, lo_in, ro_in,
    kv_in, len_in, start_in,
    hid_out, mlp_out, kv_out,
    tok, gain, pgain, w, wo, kvc, lens, starts,
    lbuf, rq, rkv, lob, rob,
    lsend, lgat, pagat, pbgat, zgat, rbig, rmat, losib,
    normed, proj, qs, kx, vx, score, prob, att, attboth, keep, ysend, yall, csa, csb, cra, crb,
    loc, lsend_sem, lrecv_sem, asend_sem, arecv_sem, psend_sem, precv_sem, zsend_sem, zrecv_sem,
    sib_send, sib_recv, ysend_sem, yrecv_sem, csend_sem, crecv_sem,
    gsend_sem, grecv_sem, fsend_sem, frecv_sem,
):
    dp = lax.axis_index("dp")
    tp = lax.axis_index("tensor")
    chip = tp // 2
    core = tp % 2
    zlo = chip // XS
    xpos = chip % XS
    yrow = dp // 4
    zhi = dp % 4
    lane8 = tp % 8
    sib = tp + 1 - 2 * core
    other = 1 - core
    ys = [(yrow + d) % 4 * 4 for d in range(4)]
    zs = [(zhi + d) % 4 for d in range(4)]
    xs = [(xpos + d) % XS for d in range(XS)]
    zlos = [zlo, 1 - zlo]
    cores = [core, other]
    zstep = jnp.where(zlo == 0, zs[3], zs[1])
    pend = {}

    def finish():
        for wait in pend.values():
            wait()

    barrier = pltpu.get_barrier_semaphore()

    def greet(device):
        pl.semaphore_signal(barrier, inc=1, device_id=device, device_id_type=MESH)

    for dz, copy_at in ((2, zlos[1]), (1, 0), (3, 1), (0, zlo)):
        for dy in (2, 1, 3, 0):
            if dz or dy:
                greet({"dp": ys[dy] + zs[dz], "tensor": copy_at * 8 + lane8})
    for dz in (2, 1, 3):
        greet({"dp": ys[0] + zs[dz]})
    group = [(z, x, c) for x in (2, 1, 3, 0) for z in (1, 0) for c in (0, 1)][:-2]
    group = [p for p in group if any(p)] + [(0, 0, 1)]

    def member(p):
        return zlos[p[0]] * 8 + xs[p[1]] * 2 + cores[p[2]]

    for p in group:
        greet({"tensor": member(p)})

    def load(name, src, dst):
        c = pltpu.make_async_copy(src, dst, loc.at[len(pend)])
        c.start()
        pend[name] = c.wait

    def ready(*names):
        for name in names:
            pend.pop(name)()

    active = jnp.logical_or(zlo == 0, core == 0)
    slab = jnp.where(zlo == 0, lane8, 8 + lane8 // 2)
    mine = core * HALF + xpos * BLOCK
    rows = pl.ds(pl.multiple_of(16 * (lane8 % 4), 16), 16)
    load("l0", lqkv_in.at[lane8 // 4, rows], lbuf.at[0])
    load("l1", lqkv_in.at[2, pl.ds(pl.multiple_of(16 * (lane8 // 2), 16), 16)], lbuf.at[1])
    load("rq", rq_in, rq)
    load("rkv", rkv_in, rkv)
    load("lo", lo_in, lob)
    load("ro", ro_in.at[:, pl.ds(pl.multiple_of(mine, 128), BLOCK)], rob)
    load("tok", tok_in, tok)
    load("gain", gain_in, gain)
    load("len", len_in, lens)
    load("start", start_in, starts)
    step = WIDTH // 4
    for i in range(4):
        rs = pl.ds(i * step, step)
        load(("wq", i), wq_in.at[rs], w.at[rs, 0:256])
        load(("wk", i), wk_in.at[rs], w.at[rs, 256:384])
        load(("wv", i), wv_in.at[rs], w.at[rs, 384:512])
    load("k", kv_in.at[0, :, 0], kvc.at[0])
    load("v", kv_in.at[1, :, 0], kvc.at[1])
    load("wo", wo_in.at[:, pl.ds(pl.multiple_of(core * HALF, 128), HALF)], wo.at[0:256])
    load("pgain", pgain_in, pgain)

    ready("l0", "l1")
    for k in range(2):
        rank_rows = jnp.concatenate([lbuf[k], jnp.zeros((16, LPAD - LROWS), F32)], 1)
        rank_rows = jnp.where(dp % 2 == 1, pltpu.roll(rank_rows, LPAD - LROWS, 1), rank_rows)
        lsend[k] = rank_rows.astype(BF16)
    lgat[dp] = lsend[zlo]

    pl.semaphore_wait(barrier, 15 + 15 + 3)

    def each_l(f):
        def to(k, dy, dp_z, to_zlo):
            if k or dy:
                f(pltpu.make_async_remote_copy(
                    lsend.at[to_zlo], lgat.at[dp], lsend_sem.at[4 * k + dy], lrecv_sem.at[dp],
                    device_id={"dp": ys[dy] + dp_z, "tensor": to_zlo * 8 + lane8},
                    device_id_type=MESH))

        @pl.when(jnp.logical_or(zlo == 1, core == 0))
        def _():
            for k, z in ((3, zs[2]), (2, zstep)):
                for dy in (2, 1, 3, 0):
                    to(k, dy, z, zlos[1])

        @pl.when(active)
        def _():
            for k, z in ((1, zstep), (0, zhi)):
                for dy in (2, 1, 3, 0):
                    to(k, dy, z, zlo)

    def got_l():
        @pl.when(active)
        def _():
            for dz in (0, 1, 3, 2):
                for dy in (0, 1, 3, 2):
                    if dz or dy:
                        who = ys[dy] + zs[dz]
                        pltpu.make_async_copy(lgat.at[who], lgat.at[who], lrecv_sem.at[who]).wait()

    each_l(lambda c: c.start())
    pend["L", "sent"] = lambda: each_l(lambda c: c.wait_send())
    pend["L"] = got_l

    def ring(name, buf, send, recv, along_y):
        copies, waits = [], []
        for d in range(1, 4):
            if along_y:
                to = ys[d] + zhi
                src, came = buf.at[pl.ds(ys[0], 4)], buf.at[pl.ds(ys[4 - d], 4)]
            else:
                to = ys[0] + zs[d]
                src, came = buf.at[dp], buf.at[ys[0] + zs[4 - d]]
            k = d + 4 * along_y
            c = pltpu.make_async_remote_copy(
                src, src, send.at[k], recv.at[k], device_id={"dp": to}, device_id_type=MESH)
            copies.append(c)
            waits.append(pltpu.make_async_copy(came, came, recv.at[k]))
        for d in (2, 1, 3):
            copies[d - 1].start()
        pend[name, "sent"] = lambda: [c.wait_send() for c in copies]
        pend[name] = lambda: [c.wait() for c in waits]

    def when_active(f):
        @pl.when(active)
        def _():
            f()

    ready("rq", "rkv")
    tiles = [rq[:, 0:128], rq[:, 128:256], rkv[0], rkv[1]]
    pagat[dp] = jnp.concatenate(tiles, 0).astype(BF16)
    ring("Az", pagat, asend_sem, arecv_sem, False)
    ready("lo", "ro")
    tiles = [lob[:, 0:128], lob[:, 128:256]]
    tiles += [rob[:, 128 * i : 128 * (i + 1)] for i in range(5)]
    tiles += [jnp.zeros((4, 128), F32)]
    pbgat[dp] = jnp.concatenate(tiles, 0).astype(BF16)
    ring("Bz", pbgat, psend_sem, precv_sem, False)

    def to_sib(src, dst, k, name):
        c = pltpu.make_async_remote_copy(
            src, dst, sib_send.at[k], sib_recv.at[k],
            device_id={"tensor": sib}, device_id_type=MESH)
        c.start()
        pend[name, "sent"] = c.wait_send
        pend[name] = c.wait_recv

    to_sib(wo_in.at[:, pl.ds(pl.multiple_of(other * HALF, 128), HALF)], wo.at[256:512], 0, "wosib")


    ready("tok", "gain")
    sq = jnp.zeros((2, ROWS, 1), F32)
    for i in range(8):
        v = tok[:, :, i * 640 : (i + 1) * 640].astype(F32)
        sq = sq + jnp.sum(v * v, -1, keepdims=True)
    rs = lax.rsqrt(sq * (1.0 / WIDTH) + 1e-06)
    for i in range(8):
        cols = slice(i * 640, (i + 1) * 640)
        v = tok[:, :, cols].astype(F32) * rs * gain[:, cols][None]
        normed[:, cols] = v.reshape(2 * ROWS, 640).astype(BF16)

    acc = None
    for i in range(2):
        ready(("wq", i), ("wk", i), ("wv", i))
        part = dot(normed[:, i * step : (i + 1) * step], w[i * step : (i + 1) * step, :])
        acc = part if acc is None else acc + part
    proj[...] = acc

    ready("Az")
    ring("A", pagat, asend_sem, arecv_sem, True)
    ready("L")

    def zcopy(k):
        return pltpu.make_async_remote_copy(
            zgat.at[slab], zgat.at[slab], zsend_sem.at[k], zrecv_sem.at[slab],
            device_id={"tensor": member(group[k])}, device_id_type=MESH)

    @pl.when(active)
    def _():
        parts = []
        for j in range(0, DP, 2):
            parts += [lgat[j, :, 0:256], lgat[j, :, 256:384] + lgat[j + 1, :, 0:128]]
            parts += [lgat[j + 1, :, 128:384]]
        z = dot(jnp.concatenate(parts, 1), normed[...], NT)
        z = jnp.concatenate([z, jnp.zeros((16, 128 - 2 * ROWS), F32)], 1)
        zgat[slab] = z.astype(BF16)

        for k in range(TP - 1):
            zcopy(k).start()

    def sent_z():
        @pl.when(active)
        def _():
            for k in range(TP - 1):
                zcopy(k).wait_send()

    def got_z():
        def got(s, _):
            src = jnp.where(s < 8, s, 2 * s - 8)

            @pl.when(src != tp)
            def _():
                pltpu.make_async_copy(zgat.at[s], zgat.at[s], zrecv_sem.at[s]).wait()

            return 0

        lax.fori_loop(0, 12, got, 0)

    pend["Z", "sent"] = sent_z
    pend["Z"] = got_z
    ready("Bz")
    ring("B", pbgat, psend_sem, precv_sem, True)
    acc = proj[...]
    for i in range(2, 4):
        ready(("wq", i), ("wk", i), ("wv", i))
        acc = acc + dot(normed[:, i * step : (i + 1) * step], w[i * step : (i + 1) * step, :])
    proj[...] = acc

    ready("len", "start")
    lenf = lens[...].astype(F32)
    stf = starts[...].astype(F32)

    def column(values, rows, owner):
        hit = owner(iota((rows, ROWS), 0)) == iota((rows, ROWS), 1)
        return jnp.sum(jnp.where(hit, values, 0.0), -1, keepdims=True)

    row = iota((2 * ROWS, 1), 0)
    pos = column(lenf, 2 * ROWS, lambda r: r % ROWS) + jnp.where(row >= ROWS, 1.0, 0.0)
    lane = iota((1, HEAD), 1)
    freq = jnp.exp((lane % 64).astype(F32) * (-2.0 * math.log(1000000.0) / HEAD))
    angle = pos * freq
    cos = jnp.cos(angle)
    sin = jnp.sin(angle) * jnp.where(lane < 64, -1.0, 1.0)

    def rope(v):
        return v * cos + pltpu.roll(v, 64, 1) * sin

    arow = iota((4 * ROWS, 1), 0)
    tokstep = jnp.where(arow % 4 >= 2, 1.0, 0.0)
    alen = column(lenf, 4 * ROWS, lambda r: r // 4)
    ast = column(stf, 4 * ROWS, lambda r: r // 4)
    slot = iota((4 * ROWS, SLOTS), 1).astype(F32) - ast
    slot = jnp.where(slot < 0, slot + float(SLOTS), slot)
    visible = jnp.logical_and(slot < alen, alen + tokstep - slot < float(WINDOW))

    ready("A")
    o = iota((256, 256), 0)
    perm = one_hot(iota((256, 256), 1) == ((o % 64) // 4) * 16 + 4 * (o // 64) + o % 4)
    right = dot(perm, pagat[...].reshape(256, 128)).astype(BF16)
    rbig[...] = jnp.zeros_like(rbig)
    for t, p in enumerate((0, 0, 1, 2)):
        rbig[64 * p : 64 * (p + 1), 128 * t : 128 * (t + 1)] = right[64 * t : 64 * (t + 1)]

    ready(("L", "sent"), ("Az", "sent"), ("wosib", "sent"))
    ready("Z")
    delta = dot(zgat[...].reshape(3 * RANK, 128), rbig[...], TN)[: 2 * ROWS]
    delta = proj[...] + 0.5 * delta
    cols = [delta[:, 128 * t : 128 * (t + 1)] for t in range(4)]
    rounded = [rope(cols[0]), rope(cols[1]), rope(cols[2]), cols[3]]
    rounded = [v.astype(BF16).astype(F32) for v in rounded]
    for t in range(2):
        rows = slice(t * ROWS, (t + 1) * ROWS)
        kv_out[t, 0] = rounded[2][rows].astype(BF16)
        kv_out[t, 1] = rounded[3][rows].astype(BF16)
        for g in range(2):
            qs[pl.ds(2 * t + g, ROWS, stride=4), :] = rounded[g][rows]
        for r in range(4):
            kx[t, pl.ds(r, ROWS, stride=4), :] = rounded[2][rows]
            vx[t, pl.ds(r, ROWS, stride=4), :] = rounded[3][rows]

    scale = 1.0 / math.sqrt(HEAD)
    ready("k")
    which = iota((16, 1), 0) // 4
    odd = which % 2 == 1
    for i in range(6):
        q = qs[16 * i : 16 * (i + 1), :]
        q = jnp.concatenate([jnp.where(odd, 0.0, q), jnp.where(odd, q, 0.0)], 1).astype(BF16)
        k = [jnp.concatenate([kvc[0, 4 * i + b], kvc[0, 4 * i + b + 1]], 1) for b in (0, 2)]
        score[16 * i : 16 * (i + 1), :] = jnp.where(which < 2, dot(q, k[0], NT), dot(q, k[1], NT))
    sc = jnp.where(visible, score[...] * scale, -1e30)
    q = qs[...]
    f0 = jnp.sum(q * kx[0], -1, keepdims=True) * scale
    f1 = jnp.sum(q * kx[1], -1, keepdims=True) * scale
    f1 = jnp.where(tokstep > 0.5, f1, -1e30)
    top = jnp.maximum(jnp.max(sc, -1, keepdims=True), jnp.maximum(f0, f1))
    ex = jnp.exp(sc - top)
    e0 = jnp.exp(f0 - top)
    e1 = jnp.exp(f1 - top)
    den = jnp.sum(ex, -1, keepdims=True) + (e0 + e1)
    prob[...] = (ex / den).astype(BF16)
    p0 = (e0 / den).astype(BF16).astype(F32)
    p1 = (e1 / den).astype(BF16).astype(F32)
    att[...] = p0 * vx[0] + p1 * vx[1]
    ready("v")
    for i in range(6):
        rows = slice(16 * i, 16 * (i + 1))
        p = prob[rows, :]
        v = [jnp.concatenate([kvc[1, 4 * i + b], kvc[1, 4 * i + b + 1]], 1) for b in (0, 2)]
        s = jnp.where(which < 2, dot(p, v[0]), dot(p, v[1]))
        att[rows, :] = att[rows, :] + jnp.where(odd, s[:, 128:256], s[:, 0:128])
    heads = []
    for g in range(2):
        heads.append(jnp.concatenate([att[pl.ds(2 * t + g, ROWS, stride=4), :] for t in range(2)], 0))
    attboth[0] = jnp.concatenate(heads, 1).astype(BF16)

    to_sib(attboth.at[0], attboth.at[1], 1, "att")
    ready("B")
    grp = pbgat[:, 0:16, :].reshape(256, 128)
    rmat[0] = dot(perm, grp).astype(BF16)
    losib[0] = rmat[0, 0:128, :]
    to_sib(losib.at[0], losib.at[1], 2, "losib")
    grp = pbgat[:, 16:32, :].reshape(256, 128)
    rmat[1] = dot(perm, grp).astype(BF16)

    offsets = ((1, 2), (0, 2), (1, 1), (1, 3), (0, 1), (0, 3), (1, 0))

    def at(o):
        return zlos[o[0]] * XS + xs[o[1]]

    def source(o):
        return zlos[o[0]] * XS + xs[-o[1]]

    def ccopy(c, h):
        send, recv = (csa, cra) if h == 0 else (csb, crb)
        return pltpu.make_async_remote_copy(
            send.at[c], recv.at[chip], csend_sem.at[h, c], crecv_sem.at[h, chip],
            device_id={"tensor": 2 * c + core}, device_id_type=MESH)

    def ycopy(c):
        return pltpu.make_async_remote_copy(
            ysend.at[c // XS], yall.at[chip], ysend_sem.at[c], yrecv_sem.at[chip],
            device_id={"tensor": 2 * c + core}, device_id_type=MESH)

    ready("wo")
    own = attboth[0]
    for h, (first, width) in enumerate(PARTS):
        for n in (2, 1, 3, 0):
            cols = pl.ds(pl.multiple_of(xs[n] * BLOCK + first, 128), width)
            keep[n, :, first : first + width] = dot(own, wo[0:256, cols])
    ready("wosib", "att")
    theirs = attboth[1]
    total = []
    for h, (first, width) in enumerate(PARTS):
        for n in (2, 1, 3, 0):
            x = xs[n]
            cols = pl.ds(pl.multiple_of(x * BLOCK + first, 128), width)
            part = keep[n, :, first : first + width] + dot(theirs, wo[256:512, cols])
            for t in range(2):
                (csa, csb)[h][t * XS + x] = part[t * ROWS : (t + 1) * ROWS].astype(BF16)
            ccopy(zlos[1] * XS + x, h).start()
            if n != 0:
                ccopy(zlo * XS + x, h).start()
            else:
                total.append(jnp.where(zlo == 0, part[0:ROWS], part[ROWS:]))
        if h == 0:
            ready("losib")
            lot = [jnp.concatenate([losib[k, 0:64], losib[k, 64:128]], 1) for k in range(2)]
            y = dot(own, lot[0], NT) + dot(theirs, lot[1], NT)
            y = jnp.concatenate([y, jnp.zeros((2 * ROWS, 128 - RANK), F32)], 1)
            ysend[0] = y[0:ROWS].astype(BF16)
            ysend[1] = y[ROWS:].astype(BF16)
            for o in offsets:
                ycopy(at(o)).start()
    pend["Y", "sent"] = lambda: [ycopy(at(o)).wait_send() for o in offsets]
    pend["C", "sent"] = lambda: [ccopy(at(o), h).wait_send() for o in offsets for h in range(2)]

    ready(("A", "sent"), ("Bz", "sent"), ("B", "sent"), ("Z", "sent"), ("att", "sent"))
    ready(("losib", "sent"))
    ysum = jnp.where(zlo == 0, y[0:ROWS], y[ROWS:])
    for o in offsets[::-1]:
        src = source(o)
        pltpu.make_async_copy(yall.at[src], yall.at[src], yrecv_sem.at[src]).wait()
        ysum = ysum + yall[src].astype(F32)
    ysum = (0.5 * ysum[:, 0:RANK]).astype(BF16)
    ro = jnp.concatenate(
        [rmat[0, 128:192, :], rmat[0, 192:256, :], rmat[1, 0:64, :], rmat[1, 64:128, :],
         rmat[1, 128:192, :]], 1)

    def block(k, c, h):
        return hid_out.at[c // XS, :, pl.ds(
            pl.multiple_of(k * HALF + c % XS * BLOCK + PARTS[h][0], 128), PARTS[h][1])]

    def gcopy(c, h):
        return pltpu.make_async_remote_copy(
            block(core, chip, h), block(core, chip, h), gsend_sem.at[h, c], grecv_sem.at[h, chip],
            device_id={"tensor": 2 * c + core}, device_id_type=MESH)

    def fcopy(c, h):
        return pltpu.make_async_remote_copy(
            block(core, c, h), block(core, c, h), fsend_sem.at[h, c], frecv_sem.at[h, c],
            device_id={"tensor": sib}, device_id_type=MESH)

    def squares(v):
        v = v.astype(F32)
        v = v * v
        return sum(v[:, i : i + 128] for i in range(0, v.shape[1], 128))

    sq = [jnp.zeros((ROWS, 128), F32) for _ in range(2)]
    for h, (first, width) in enumerate(PARTS):
        here = pl.ds(pl.multiple_of(mine + first, 128), width)
        out = total[h] + tok[zlo, :, here].astype(F32) + dot(ysum, ro[:, first : first + width])
        recv = (cra, crb)[h]
        for o in offsets[::-1]:
            src = source(o)
            pltpu.make_async_copy(recv.at[src], recv.at[src], crecv_sem.at[h, src]).wait()
            out = out + recv[src].astype(F32)
        out = out.astype(BF16)
        hid_out[zlo, :, here] = out
        sq[0] = sq[0] + squares(out)
        for o in offsets:
            gcopy(at(o), h).start()
        fcopy(chip, h).start()
    pend["G", "sent"] = lambda: [gcopy(at(o), h).wait_send() for o in offsets for h in range(2)]
    every = ((0, 0),) + offsets[::-1]
    ready(("Y", "sent"), ("C", "sent"))
    pend["F", "sent"] = lambda: [fcopy(source(o), h).wait_send() for o in every for h in range(2)]
    for h in range(2):
        for o in offsets[::-1]:
            mark = block(core, source(o), h)
            pltpu.make_async_copy(mark, mark, grecv_sem.at[h, source(o)]).wait()
            fcopy(source(o), h).start()
            sq[o[0]] = sq[o[0]] + squares(mark[...])
    ready(("G", "sent"))
    for h in range(2):
        for o in every:
            mark = block(other, source(o), h)
            pltpu.make_async_copy(mark, mark, frecv_sem.at[h, source(o)]).wait()
            sq[o[0]] = sq[o[0]] + squares(mark[...])

    ready("pgain")
    for t in range(2):
        mean = jnp.sum(jnp.where(zlo == t, sq[0], sq[1]), -1, keepdims=True) * (1.0 / WIDTH)
        rs = lax.rsqrt(mean + 1e-06)
        for i in range(8):
            cols = slice(i * 640, (i + 1) * 640)
            mlp_out[t, :, cols] = (hid_out[t, :, cols].astype(F32) * rs * pgain[:, cols]).astype(BF16)

    finish()


def close_kernel(hid_ref, mlp_ref, kv_ref, hid_out, mlp_out, kv_out, sems):
    copies = []
    for k, (src, dst) in enumerate(((hid_ref, hid_out), (mlp_ref, mlp_out), (kv_ref, kv_out))):
        copies.append(pltpu.make_async_copy(src, dst, sems.at[k]))
    for c in copies:
        c.start()
    for c in copies:
        c.wait()


def shards(
    tokens_in, attn_gain, post_gain, w_query, key_weight_base, value_weight_base, w_out, left_qkv,
    right_query, right_key_value, left_out, right_out, kv_cache, lengths, starts,
):
    hbm = pl.BlockSpec(memory_space=pltpu.HBM)
    vmem = pl.BlockSpec(memory_space=pltpu.VMEM)
    dma = pltpu.SemaphoreType.DMA
    scratch = [
        pltpu.VMEM((2, ROWS, WIDTH), BF16),
        pltpu.VMEM((1, WIDTH), F32),
        pltpu.VMEM((1, WIDTH), F32),
        pltpu.VMEM((WIDTH, 512), BF16),
        pltpu.VMEM((512, HALF), BF16),
        pltpu.VMEM((2, ROWS, SLOTS, HEAD), BF16),
        pltpu.VMEM((1, ROWS), jnp.int32),
        pltpu.VMEM((1, ROWS), jnp.int32),
        pltpu.VMEM((2, 16, LROWS), F32),
        pltpu.VMEM((4, 256), F32),
        pltpu.VMEM((2, 4, 128), F32),
        pltpu.VMEM((4, 256), F32),
        pltpu.VMEM((4, BLOCK), F32),
        pltpu.VMEM((2, 16, LPAD), BF16),
        pltpu.VMEM((DP, 16, LPAD), BF16),
        pltpu.VMEM((DP, 16, 128), BF16),
        pltpu.VMEM((DP, 32, 128), BF16),
        pltpu.VMEM((12, 16, 128), BF16),
        pltpu.VMEM((3 * RANK, 512), BF16),
        pltpu.VMEM((2, 256, 128), BF16),
        pltpu.VMEM((2, 128, 128), BF16),
        pltpu.VMEM((2 * ROWS, WIDTH), BF16),
        pltpu.VMEM((2 * ROWS, 512), F32),
        pltpu.VMEM((4 * ROWS, HEAD), F32),
        pltpu.VMEM((2, 4 * ROWS, HEAD), F32),
        pltpu.VMEM((2, 4 * ROWS, HEAD), F32),
        pltpu.VMEM((4 * ROWS, SLOTS), F32),
        pltpu.VMEM((4 * ROWS, SLOTS), BF16),
        pltpu.VMEM((4 * ROWS, HEAD), F32),
        pltpu.VMEM((2, 2 * ROWS, 256), BF16),
        pltpu.VMEM((XS, 2 * ROWS, BLOCK), F32),
        pltpu.VMEM((2, ROWS, 128), BF16),
        pltpu.VMEM((CHIPS, ROWS, 128), BF16),
        pltpu.VMEM((CHIPS, ROWS, PARTS[0][1]), BF16),
        pltpu.VMEM((CHIPS, ROWS, PARTS[1][1]), BF16),
        pltpu.VMEM((CHIPS, ROWS, PARTS[0][1]), BF16),
        pltpu.VMEM((CHIPS, ROWS, PARTS[1][1]), BF16),
        dma((32,)),
        dma((DP,)), dma((DP,)), dma((8,)), dma((8,)), dma((8,)), dma((8,)),
        dma((TP,)), dma((12,)), dma((3,)), dma((3,)),
        dma((CHIPS,)), dma((CHIPS,)), dma((2, CHIPS)), dma((2, CHIPS)),
        dma((2, CHIPS)), dma((2, CHIPS)), dma((2, CHIPS)), dma((2, CHIPS)),
    ]
    shapes = (
        jax.ShapeDtypeStruct((2, ROWS, WIDTH), BF16),
        jax.ShapeDtypeStruct((2, ROWS, WIDTH), BF16),
        jax.ShapeDtypeStruct((2, 2, ROWS, HEAD), BF16),
    )
    args = (
        tokens_in, attn_gain.reshape(1, WIDTH), post_gain.reshape(1, WIDTH), w_query,
        key_weight_base, value_weight_base, w_out, left_qkv.swapaxes(1, 2), right_query,
        right_key_value, left_out.T, right_out, kv_cache, lengths.reshape(1, ROWS),
        starts.reshape(1, ROWS),
    )
    results = pl.pallas_call(
        main_kernel,
        out_shape=tuple(pltpu.VMEM(s.shape, s.dtype) for s in shapes),
        in_specs=[hbm] * len(args),
        out_specs=(vmem, vmem, vmem),
        scratch_shapes=scratch,
        compiler_params=pltpu.CompilerParams(
            collective_id=0, has_side_effects=True, vmem_limit_bytes=40 * 1024 * 1024),
    )(*[pltpu.with_memory_space_constraint(a, pltpu.HBM) for a in args])
    return pl.pallas_call(
        close_kernel,
        out_shape=shapes,
        in_specs=[vmem] * 3,
        out_specs=(hbm, hbm, hbm),
        scratch_shapes=[dma((3,))],
    )(*[pltpu.with_memory_space_constraint(a, pltpu.VMEM) for a in results])


def solution(mesh):
    in_specs = (
        P(None, "dp", None),
        P(),
        P(),
        P(None, "tensor"),
        P(None, "tensor"),
        P(None, "tensor"),
        P("tensor", None),
        P(None, "dp", None),
        P("dp", "tensor"),
        P(None, "dp", "tensor"),
        P("tensor", "dp"),
        P("dp", None),
        P(None, "dp", "tensor", None, None),
        P("dp"),
        P("dp"),
    )
    out_specs = (P(None, "dp", None), P(None, "dp", None), P(None, None, "dp", "tensor"))
    return jax.shard_map(shards, mesh=mesh, in_specs=in_specs, out_specs=out_specs, check_vma=False)
```

time: 43.8 us -> 41.2 us (0.941)
  Pallas kernels: 43.1 us -> 40.5 us
    pallas_call x1, Pallas kernels: 42.1 us -> 39.5 us  [shards(): pl.pallas_call(main_kernel, out_shape=tuple((pltpu.VMEM(s.shape, s.dtype)...]
where the time goes in v3:
time: 41.2 us; the launch traced here: 41.1 us
  Pallas kernels  40.5 us (98%)
  between operations  0.64 us (2%)
    pallas_call x1, Pallas kernels, shards(): pl.pallas_call(main_kernel, out_shape=tuple((pltpu.VMEM(s.shape, s.dtype)...  39.5 us
    pallas_call x1, Pallas kernels, shards(): pl.pallas_call(close_kernel, out_shape=shapes, in_specs=[vmem] * 3, out_s...  0.97 us

profile of v3, /device:TPU:1, one launch (start us, length us, event | category | flops | bytes accessed | tf_op | source)
XLA Modules:
  0.0 41.1 jit_solution(1721652687945771831)
XLA Ops:
  0.6 39.5 %shard_map.166 = (bf16[2,24,5120]{2,1,0:T(8,128)(2,1)S(1)}, bf16[2,24,5120]{2,1,0:T(8,128)(2,1)S(1)}, bf16[2,2,24,128]{3,2,1,0:T(8,128)(2,1)S(1)}) custom-call(bf16[2,24,5120]{2,1,0:T(8,128)(2,1)} %tok_in.1, f32[1,5120]{1,0:T(1,128)} %bitcast.7, f32[1,5120]{1,0:T(1,128)} %bitcast.8, bf16[5120,256]{1,0:T(8,128)(2,1)} %wq_in.1, bf16[5120,128]{1,0:T(8,128)(2,1)} %wk_in.1, ...), custom_call_target="tpu_custom_call" | custom-call | tf_op jit(solution)/shard_map/pallas_call | solution.py:585
  40.1 1.0 %shard_map.167 = (bf16[2,24,5120]{2,1,0:T(8,128)(2,1)}, bf16[2,24,5120]{2,1,0:T(8,128)(2,1)}, bf16[2,2,24,128]{3,2,1,0:T(8,128)(2,1)}) custom-call(bf16[2,24,5120]{2,1,0:T(8,128)(2,1)S(1)} %get-tuple-element.6.hid_ref, bf16[2,24,5120]{2,1,0:T(8,128)(2,1)S(1)} %get-tuple-element.7.mlp_ref, bf16[2,2,24,128]{3,2,1,0:T(8,128)(2,1)S(1)} %get-tuple-element.8.kv_ref), custom_call_target="tpu_custom_call" | custom-call | tf_op jit(solution)/shard_map/pallas_call | solution.py:594

commit v4 on v3

--- a/solution.py
+++ b/solution.py
@@ -23,7 +23,7 @@
 XS = 4
 HALF = WIDTH // 2
 BLOCK = HALF // XS
-PARTS = ((0, 256), (256, 384))
+PARTS = ((0, 384), (384, 256))
 LROWS = WIDTH // DP
 LPAD = 384
 NT = (((1,), (1,)), ((), ()))
@@ -46,11 +46,11 @@
 def main_kernel(
     tok_in, gain_in, pgain_in, wq_in, wk_in, wv_in, wo_in, lqkv_in, rq_in, rkv_in, lo_in, ro_in,
     kv_in, len_in, start_in,
-    hid_out, mlp_out, kv_out,
-    tok, gain, pgain, w, wo, kvc, lens, starts,
+    hid_out, sq_out, pgain, kv_out,
+    tok, gain, w, wo, kvc, lens, starts,
     lbuf, rq, rkv, lob, rob,
-    lsend, lgat, pagat, pbgat, zgat, rbig, rmat, losib,
-    normed, proj, qs, kx, vx, score, prob, att, attboth, keep, ysend, yall, csa, csb, cra, crb,
+    lsend, lgat, pagat, pbgat, zgat, rbig, rmat,
+    normed, proj, qs, kx, vx, score, prob, att, attboth, keep, ysend, yall, csend, crecv,
     loc, lsend_sem, lrecv_sem, asend_sem, arecv_sem, psend_sem, precv_sem, zsend_sem, zrecv_sem,
     sib_send, sib_recv, ysend_sem, yrecv_sem, csend_sem, crecv_sem,
     gsend_sem, grecv_sem, fsend_sem, frecv_sem,
@@ -376,13 +376,28 @@
     attboth[0] = jnp.concatenate(heads, 1).astype(BF16)
 
     to_sib(attboth.at[0], attboth.at[1], 1, "att")
+    own = attboth[0]
     ready("B")
-    grp = pbgat[:, 0:16, :].reshape(256, 128)
-    rmat[0] = dot(perm, grp).astype(BF16)
-    losib[0] = rmat[0, 0:128, :]
-    to_sib(losib.at[0], losib.at[1], 2, "losib")
-    grp = pbgat[:, 16:32, :].reshape(256, 128)
-    rmat[1] = dot(perm, grp).astype(BF16)
+    rmat[0] = dot(perm, pbgat[:, 0:16, :].reshape(256, 128)).astype(BF16)
+    lot = jnp.concatenate([rmat[0, 0:64], rmat[0, 64:128]], 1)
+    y = dot(own, lot, NT)
+    y = jnp.concatenate([y, jnp.zeros((2 * ROWS, 128 - RANK), F32)], 1)
+    ysend[0] = y[0:ROWS].astype(BF16)
+    ysend[1] = y[ROWS:].astype(BF16)
+
+    def ycopy(k):
+        return pltpu.make_async_remote_copy(
+            ysend.at[zlos[group[k][0]]], yall.at[tp], ysend_sem.at[k], yrecv_sem.at[tp],
+            device_id={"tensor": member(group[k])}, device_id_type=MESH)
+
+    for k in range(TP - 1):
+        ycopy(k).start()
+    pend["Y", "sent"] = lambda: [ycopy(k).wait_send() for k in range(TP - 1)]
+
+    ready("wo")
+    for n in (2, 1, 3, 0):
+        cols = pl.ds(pl.multiple_of(xs[n] * BLOCK, 128), PARTS[0][1])
+        keep[n] = dot(own, wo[0:256, cols])
 
     offsets = ((1, 2), (0, 2), (1, 1), (1, 3), (0, 1), (0, 3), (1, 0))
 
@@ -393,54 +408,34 @@
         return zlos[o[0]] * XS + xs[-o[1]]
 
     def ccopy(c, h):
-        send, recv = (csa, cra) if h == 0 else (csb, crb)
+        cols = pl.ds(*PARTS[h])
         return pltpu.make_async_remote_copy(
-            send.at[c], recv.at[chip], csend_sem.at[h, c], crecv_sem.at[h, chip],
+            csend.at[c, :, cols], crecv.at[chip, :, cols], csend_sem.at[h, c], crecv_sem.at[h, chip],
             device_id={"tensor": 2 * c + core}, device_id_type=MESH)
 
-    def ycopy(c):
-        return pltpu.make_async_remote_copy(
-            ysend.at[c // XS], yall.at[chip], ysend_sem.at[c], yrecv_sem.at[chip],
-            device_id={"tensor": 2 * c + core}, device_id_type=MESH)
-
-    ready("wo")
-    own = attboth[0]
-    for h, (first, width) in enumerate(PARTS):
-        for n in (2, 1, 3, 0):
-            cols = pl.ds(pl.multiple_of(xs[n] * BLOCK + first, 128), width)
-            keep[n, :, first : first + width] = dot(own, wo[0:256, cols])
     ready("wosib", "att")
     theirs = attboth[1]
+    both = jnp.concatenate([own, theirs], 1)
     total = []
     for h, (first, width) in enumerate(PARTS):
         for n in (2, 1, 3, 0):
             x = xs[n]
             cols = pl.ds(pl.multiple_of(x * BLOCK + first, 128), width)
-            part = keep[n, :, first : first + width] + dot(theirs, wo[256:512, cols])
+            part = keep[n] + dot(theirs, wo[256:512, cols]) if h == 0 else dot(both, wo[:, cols])
             for t in range(2):
-                (csa, csb)[h][t * XS + x] = part[t * ROWS : (t + 1) * ROWS].astype(BF16)
+                csend[t * XS + x, :, first : first + width] = part[t * ROWS : (t + 1) * ROWS].astype(BF16)
             ccopy(zlos[1] * XS + x, h).start()
             if n != 0:
                 ccopy(zlo * XS + x, h).start()
             else:
                 total.append(jnp.where(zlo == 0, part[0:ROWS], part[ROWS:]))
-        if h == 0:
-            ready("losib")
-            lot = [jnp.concatenate([losib[k, 0:64], losib[k, 64:128]], 1) for k in range(2)]
-            y = dot(own, lot[0], NT) + dot(theirs, lot[1], NT)
-            y = jnp.concatenate([y, jnp.zeros((2 * ROWS, 128 - RANK), F32)], 1)
-            ysend[0] = y[0:ROWS].astype(BF16)
-            ysend[1] = y[ROWS:].astype(BF16)
-            for o in offsets:
-                ycopy(at(o)).start()
-    pend["Y", "sent"] = lambda: [ycopy(at(o)).wait_send() for o in offsets]
-    pend["C", "sent"] = lambda: [ccopy(at(o), h).wait_send() for o in offsets for h in range(2)]
+    rmat[1] = dot(perm, pbgat[:, 16:32, :].reshape(256, 128)).astype(BF16)
+    pend["C", "sent"] = lambda: [ccopy(at(o), h).wait_send() for o in offsets for h in range(len(PARTS))]
 
     ready(("A", "sent"), ("Bz", "sent"), ("B", "sent"), ("Z", "sent"), ("att", "sent"))
-    ready(("losib", "sent"))
     ysum = jnp.where(zlo == 0, y[0:ROWS], y[ROWS:])
-    for o in offsets[::-1]:
-        src = source(o)
+    for p in group[::-1]:
+        src = member(p)
         pltpu.make_async_copy(yall.at[src], yall.at[src], yrecv_sem.at[src]).wait()
         ysum = ysum + yall[src].astype(F32)
     ysum = (0.5 * ysum[:, 0:RANK]).astype(BF16)
@@ -471,29 +466,30 @@
     for h, (first, width) in enumerate(PARTS):
         here = pl.ds(pl.multiple_of(mine + first, 128), width)
         out = total[h] + tok[zlo, :, here].astype(F32) + dot(ysum, ro[:, first : first + width])
-        recv = (cra, crb)[h]
+        cols = pl.ds(first, width)
         for o in offsets[::-1]:
             src = source(o)
-            pltpu.make_async_copy(recv.at[src], recv.at[src], crecv_sem.at[h, src]).wait()
-            out = out + recv[src].astype(F32)
+            mark = crecv.at[src, :, cols]
+            pltpu.make_async_copy(mark, mark, crecv_sem.at[h, src]).wait()
+            out = out + mark[...].astype(F32)
         out = out.astype(BF16)
         hid_out[zlo, :, here] = out
         sq[0] = sq[0] + squares(out)
         for o in offsets:
             gcopy(at(o), h).start()
         fcopy(chip, h).start()
-    pend["G", "sent"] = lambda: [gcopy(at(o), h).wait_send() for o in offsets for h in range(2)]
+    pend["G", "sent"] = lambda: [gcopy(at(o), h).wait_send() for o in offsets for h in range(len(PARTS))]
     every = ((0, 0),) + offsets[::-1]
     ready(("Y", "sent"), ("C", "sent"))
-    pend["F", "sent"] = lambda: [fcopy(source(o), h).wait_send() for o in every for h in range(2)]
-    for h in range(2):
+    pend["F", "sent"] = lambda: [fcopy(source(o), h).wait_send() for o in every for h in range(len(PARTS))]
+    for h in range(len(PARTS)):
         for o in offsets[::-1]:
             mark = block(core, source(o), h)
             pltpu.make_async_copy(mark, mark, grecv_sem.at[h, source(o)]).wait()
             fcopy(source(o), h).start()
             sq[o[0]] = sq[o[0]] + squares(mark[...])
     ready(("G", "sent"))
-    for h in range(2):
+    for h in range(len(PARTS)):
         for o in every:
             mark = block(other, source(o), h)
             pltpu.make_async_copy(mark, mark, frecv_sem.at[h, source(o)]).wait()
@@ -501,21 +497,29 @@
 
     ready("pgain")
     for t in range(2):
-        mean = jnp.sum(jnp.where(zlo == t, sq[0], sq[1]), -1, keepdims=True) * (1.0 / WIDTH)
-        rs = lax.rsqrt(mean + 1e-06)
-        for i in range(8):
-            cols = slice(i * 640, (i + 1) * 640)
-            mlp_out[t, :, cols] = (hid_out[t, :, cols].astype(F32) * rs * pgain[:, cols]).astype(BF16)
+        sq_out[t] = jnp.where(zlo == t, sq[0], sq[1])
 
     finish()
 
 
-def close_kernel(hid_ref, mlp_ref, kv_ref, hid_out, mlp_out, kv_out, sems):
+def close_kernel(hid, sq, gain, kv, hid_out, mlp_out, kv_out, mlp, sems):
     copies = []
-    for k, (src, dst) in enumerate(((hid_ref, hid_out), (mlp_ref, mlp_out), (kv_ref, kv_out))):
-        copies.append(pltpu.make_async_copy(src, dst, sems.at[k]))
-    for c in copies:
+
+    def send(src, dst):
+        c = pltpu.make_async_copy(src, dst, sems.at[len(copies)])
         c.start()
+        copies.append(c)
+
+    send(hid, hid_out)
+    send(kv, kv_out)
+    for t in range(2):
+        rs = lax.rsqrt(jnp.sum(sq[t], -1, keepdims=True) * (1.0 / WIDTH) + 1e-06)
+        for half in range(2):
+            for i in range(4 * half, 4 * half + 4):
+                cols = slice(i * 640, (i + 1) * 640)
+                mlp[t, :, cols] = (hid[t, :, cols].astype(F32) * rs * gain[:, cols]).astype(BF16)
+            part = pl.ds(half * HALF, HALF)
+            send(mlp.at[t, :, part], mlp_out.at[t, :, part])
     for c in copies:
         c.wait()
 
@@ -529,7 +533,6 @@
     dma = pltpu.SemaphoreType.DMA
     scratch = [
         pltpu.VMEM((2, ROWS, WIDTH), BF16),
-        pltpu.VMEM((1, WIDTH), F32),
         pltpu.VMEM((1, WIDTH), F32),
         pltpu.VMEM((WIDTH, 512), BF16),
         pltpu.VMEM((512, HALF), BF16),
@@ -548,7 +551,6 @@
         pltpu.VMEM((12, 16, 128), BF16),
         pltpu.VMEM((3 * RANK, 512), BF16),
         pltpu.VMEM((2, 256, 128), BF16),
-        pltpu.VMEM((2, 128, 128), BF16),
         pltpu.VMEM((2 * ROWS, WIDTH), BF16),
         pltpu.VMEM((2 * ROWS, 512), F32),
         pltpu.VMEM((4 * ROWS, HEAD), F32),
@@ -558,24 +560,20 @@
         pltpu.VMEM((4 * ROWS, SLOTS), BF16),
         pltpu.VMEM((4 * ROWS, HEAD), F32),
         pltpu.VMEM((2, 2 * ROWS, 256), BF16),
-        pltpu.VMEM((XS, 2 * ROWS, BLOCK), F32),
+        pltpu.VMEM((XS, 2 * ROWS, PARTS[0][1]), F32),
         pltpu.VMEM((2, ROWS, 128), BF16),
-        pltpu.VMEM((CHIPS, ROWS, 128), BF16),
-        pltpu.VMEM((CHIPS, ROWS, PARTS[0][1]), BF16),
-        pltpu.VMEM((CHIPS, ROWS, PARTS[1][1]), BF16),
-        pltpu.VMEM((CHIPS, ROWS, PARTS[0][1]), BF16),
-        pltpu.VMEM((CHIPS, ROWS, PARTS[1][1]), BF16),
+        pltpu.VMEM((TP, ROWS, 128), BF16),
+        pltpu.VMEM((CHIPS, ROWS, BLOCK), BF16),
+        pltpu.VMEM((CHIPS, ROWS, BLOCK), BF16),
         dma((32,)),
         dma((DP,)), dma((DP,)), dma((8,)), dma((8,)), dma((8,)), dma((8,)),
         dma((TP,)), dma((12,)), dma((3,)), dma((3,)),
-        dma((CHIPS,)), dma((CHIPS,)), dma((2, CHIPS)), dma((2, CHIPS)),
-        dma((2, CHIPS)), dma((2, CHIPS)), dma((2, CHIPS)), dma((2, CHIPS)),
+        dma((TP,)), dma((TP,)), *[dma((len(PARTS), CHIPS))] * 6,
     ]
-    shapes = (
-        jax.ShapeDtypeStruct((2, ROWS, WIDTH), BF16),
-        jax.ShapeDtypeStruct((2, ROWS, WIDTH), BF16),
-        jax.ShapeDtypeStruct((2, 2, ROWS, HEAD), BF16),
-    )
+    hidden = ((2, ROWS, WIDTH), BF16)
+    squares = ((2, ROWS, 128), F32)
+    row = ((1, WIDTH), F32)
+    pair = ((2, 2, ROWS, HEAD), BF16)
     args = (
         tokens_in, attn_gain.reshape(1, WIDTH), post_gain.reshape(1, WIDTH), w_query,
         key_weight_base, value_weight_base, w_out, left_qkv.swapaxes(1, 2), right_query,
@@ -584,19 +582,19 @@
     )
     results = pl.pallas_call(
         main_kernel,
-        out_shape=tuple(pltpu.VMEM(s.shape, s.dtype) for s in shapes),
+        out_shape=tuple(pltpu.VMEM(*s) for s in (hidden, squares, row, pair)),
         in_specs=[hbm] * len(args),
-        out_specs=(vmem, vmem, vmem),
+        out_specs=(vmem,) * 4,
         scratch_shapes=scratch,
         compiler_params=pltpu.CompilerParams(
             collective_id=0, has_side_effects=True, vmem_limit_bytes=40 * 1024 * 1024),
     )(*[pltpu.with_memory_space_constraint(a, pltpu.HBM) for a in args])
     return pl.pallas_call(
         close_kernel,
-        out_shape=shapes,
-        in_specs=[vmem] * 3,
-        out_specs=(hbm, hbm, hbm),
-        scratch_shapes=[dma((3,))],
+        out_shape=tuple(jax.ShapeDtypeStruct(*s) for s in (hidden, hidden, pair)),
+        in_specs=[vmem] * 4,
+        out_specs=(hbm,) * 3,
+        scratch_shapes=[pltpu.VMEM(*hidden), dma((6,))],
     )(*[pltpu.with_memory_space_constraint(a, pltpu.VMEM) for a in results])
 
 

time: 41.2 us -> 40.8 us (level)
  no operation moved by 1% of the time
where the time goes in v4:
time: 40.8 us; the launch traced here: 40.7 us
  Pallas kernels  40.1 us (98%)
  between operations  0.64 us (2%)
    pallas_call x1, Pallas kernels, shards(): pl.pallas_call(main_kernel, out_shape=tuple((pltpu.VMEM(*s) for s in (hid...  39.1 us
    pallas_call x1, Pallas kernels, shards(): pl.pallas_call(close_kernel, out_shape=tuple((jax.ShapeDtypeStruct(*s) fo...  0.99 us

profile of v4, /device:TPU:1, one launch (start us, length us, event | category | flops | bytes accessed | tf_op | source)
XLA Modules:
  0.0 40.7 jit_solution(10684640898985945676)
XLA Ops:
  0.6 39.1 %shard_map.166 = (bf16[2,24,5120]{2,1,0:T(8,128)(2,1)S(1)}, f32[2,24,128]{2,1,0:T(8,128)S(1)}, f32[1,5120]{1,0:T(1,128)S(1)}, bf16[2,2,24,128]{3,2,1,0:T(8,128)(2,1)S(1)}) custom-call(bf16[2,24,5120]{2,1,0:T(8,128)(2,1)} %tok_in.1, f32[1,5120]{1,0:T(1,128)} %bitcast.7, f32[1,5120]{1,0:T(1,128)} %bitcast.8, bf16[5120,256]{1,0:T(8,128)(2,1)} %wq_in.1, ...), custom_call_target="tpu_custom_call" | custom-call | tf_op jit(solution)/shard_map/pallas_call | solution.py:583
  39.7 1.0 %shard_map.167 = (bf16[2,24,5120]{2,1,0:T(8,128)(2,1)}, bf16[2,24,5120]{2,1,0:T(8,128)(2,1)}, bf16[2,2,24,128]{3,2,1,0:T(8,128)(2,1)}) custom-call(bf16[2,24,5120]{2,1,0:T(8,128)(2,1)S(1)} %get-tuple-element.7.hid, f32[2,24,128]{2,1,0:T(8,128)S(1)} %get-tuple-element.8.sq, f32[1,5120]{1,0:T(1,128)S(1)} %get-tuple-element.9.gain, ...), custom_call_target="tpu_custom_call" | custom-call | tf_op jit(solution)/shard_map/pallas_call | solution.py:592

commit v5 on v4

--- a/solution.py
+++ b/solution.py
@@ -50,7 +50,7 @@
     tok, gain, w, wo, kvc, lens, starts,
     lbuf, rq, rkv, lob, rob,
     lsend, lgat, pagat, pbgat, zgat, rbig, rmat,
-    normed, proj, qs, kx, vx, score, prob, att, attboth, keep, ysend, yall, csend, crecv,
+    normed, proj, qs, kx, vx, score, att, attboth, keep, ysend, yall, csend, crecv,
     loc, lsend_sem, lrecv_sem, asend_sem, arecv_sem, psend_sem, precv_sem, zsend_sem, zrecv_sem,
     sib_send, sib_recv, ysend_sem, yrecv_sem, csend_sem, crecv_sem,
     gsend_sem, grecv_sem, fsend_sem, frecv_sem,
@@ -78,6 +78,22 @@
         for wait in pend.values():
             wait()
 
+    def load(name, src, dst):
+        c = pltpu.make_async_copy(src, dst, loc.at[len(pend)])
+        c.start()
+        pend[name] = c.wait
+
+    def ready(*names):
+        for name in names:
+            pend.pop(name)()
+
+    active = jnp.logical_or(zlo == 0, core == 0)
+    slab = jnp.where(zlo == 0, lane8, 8 + lane8 // 2)
+    mine = core * HALF + xpos * BLOCK
+    rows = pl.ds(pl.multiple_of(16 * (lane8 % 4), 16), 16)
+    load("l0", lqkv_in.at[lane8 // 4, rows], lbuf.at[0])
+    load("l1", lqkv_in.at[2, pl.ds(pl.multiple_of(16 * (lane8 // 2), 16), 16)], lbuf.at[1])
+
     barrier = pltpu.get_barrier_semaphore()
 
     def greet(device):
@@ -98,21 +114,6 @@
     for p in group:
         greet({"tensor": member(p)})
 
-    def load(name, src, dst):
-        c = pltpu.make_async_copy(src, dst, loc.at[len(pend)])
-        c.start()
-        pend[name] = c.wait
-
-    def ready(*names):
-        for name in names:
-            pend.pop(name)()
-
-    active = jnp.logical_or(zlo == 0, core == 0)
-    slab = jnp.where(zlo == 0, lane8, 8 + lane8 // 2)
-    mine = core * HALF + xpos * BLOCK
-    rows = pl.ds(pl.multiple_of(16 * (lane8 % 4), 16), 16)
-    load("l0", lqkv_in.at[lane8 // 4, rows], lbuf.at[0])
-    load("l1", lqkv_in.at[2, pl.ds(pl.multiple_of(16 * (lane8 // 2), 16), 16)], lbuf.at[1])
     load("rq", rq_in, rq)
     load("rkv", rkv_in, rkv)
     load("lo", lo_in, lob)
@@ -161,18 +162,8 @@
                 for dy in (2, 1, 3, 0):
                     to(k, dy, z, zlo)
 
-    def got_l():
-        @pl.when(active)
-        def _():
-            for dz in (0, 1, 3, 2):
-                for dy in (0, 1, 3, 2):
-                    if dz or dy:
-                        who = ys[dy] + zs[dz]
-                        pltpu.make_async_copy(lgat.at[who], lgat.at[who], lrecv_sem.at[who]).wait()
-
     each_l(lambda c: c.start())
     pend["L", "sent"] = lambda: each_l(lambda c: c.wait_send())
-    pend["L"] = got_l
 
     def ring(name, buf, send, recv, along_y):
         copies, waits = [], []
@@ -240,7 +231,6 @@
 
     ready("Az")
     ring("A", pagat, asend_sem, arecv_sem, True)
-    ready("L")
 
     def zcopy(k):
         return pltpu.make_async_remote_copy(
@@ -249,11 +239,20 @@
 
     @pl.when(active)
     def _():
-        parts = []
-        for j in range(0, DP, 2):
-            parts += [lgat[j, :, 0:256], lgat[j, :, 256:384] + lgat[j + 1, :, 0:128]]
-            parts += [lgat[j + 1, :, 128:384]]
-        z = dot(jnp.concatenate(parts, 1), normed[...], NT)
+        z = jnp.zeros((16, 2 * ROWS), F32)
+        for half in range(2):
+            parts, cols = [], []
+            for j in range(2 * half, DP, 4):
+                for who in (j, j + 1):
+                    @pl.when(dp != who)
+                    def _():
+                        mark = lgat.at[who]
+                        pltpu.make_async_copy(mark, mark, lrecv_sem.at[who]).wait()
+
+                parts += [lgat[j, :, 0:256], lgat[j, :, 256:384] + lgat[j + 1, :, 0:128]]
+                parts += [lgat[j + 1, :, 128:384]]
+                cols += [normed[:, LROWS * j : LROWS * (j + 2)]]
+            z = z + dot(jnp.concatenate(parts, 1), jnp.concatenate(cols, 1), NT)
         z = jnp.concatenate([z, jnp.zeros((16, 128 - 2 * ROWS), F32)], 1)
         zgat[slab] = z.astype(BF16)
 
@@ -342,13 +341,12 @@
 
     scale = 1.0 / math.sqrt(HEAD)
     ready("k")
-    which = iota((16, 1), 0) // 4
-    odd = which % 2 == 1
-    for i in range(6):
-        q = qs[16 * i : 16 * (i + 1), :]
+    odd = iota((8, 1), 0) >= 4
+    for i in range(ROWS // 2):
+        q = qs[8 * i : 8 * (i + 1), :]
         q = jnp.concatenate([jnp.where(odd, 0.0, q), jnp.where(odd, q, 0.0)], 1).astype(BF16)
-        k = [jnp.concatenate([kvc[0, 4 * i + b], kvc[0, 4 * i + b + 1]], 1) for b in (0, 2)]
-        score[16 * i : 16 * (i + 1), :] = jnp.where(which < 2, dot(q, k[0], NT), dot(q, k[1], NT))
+        k = jnp.concatenate([kvc[0, 2 * i], kvc[0, 2 * i + 1]], 1)
+        score[8 * i : 8 * (i + 1), :] = dot(q, k, NT)
     sc = jnp.where(visible, score[...] * scale, -1e30)
     q = qs[...]
     f0 = jnp.sum(q * kx[0], -1, keepdims=True) * scale
@@ -359,16 +357,15 @@
     e0 = jnp.exp(f0 - top)
     e1 = jnp.exp(f1 - top)
     den = jnp.sum(ex, -1, keepdims=True) + (e0 + e1)
-    prob[...] = (ex / den).astype(BF16)
+    score[...] = ex / den
     p0 = (e0 / den).astype(BF16).astype(F32)
     p1 = (e1 / den).astype(BF16).astype(F32)
     att[...] = p0 * vx[0] + p1 * vx[1]
     ready("v")
-    for i in range(6):
-        rows = slice(16 * i, 16 * (i + 1))
-        p = prob[rows, :]
-        v = [jnp.concatenate([kvc[1, 4 * i + b], kvc[1, 4 * i + b + 1]], 1) for b in (0, 2)]
-        s = jnp.where(which < 2, dot(p, v[0]), dot(p, v[1]))
+    for i in range(ROWS // 2):
+        rows = slice(8 * i, 8 * (i + 1))
+        v = jnp.concatenate([kvc[1, 2 * i], kvc[1, 2 * i + 1]], 1)
+        s = dot(score[rows, :].astype(BF16), v)
         att[rows, :] = att[rows, :] + jnp.where(odd, s[:, 128:256], s[:, 0:128])
     heads = []
     for g in range(2):
@@ -557,7 +554,6 @@
         pltpu.VMEM((2, 4 * ROWS, HEAD), F32),
         pltpu.VMEM((2, 4 * ROWS, HEAD), F32),
         pltpu.VMEM((4 * ROWS, SLOTS), F32),
-        pltpu.VMEM((4 * ROWS, SLOTS), BF16),
         pltpu.VMEM((4 * ROWS, HEAD), F32),
         pltpu.VMEM((2, 2 * ROWS, 256), BF16),
         pltpu.VMEM((XS, 2 * ROWS, PARTS[0][1]), F32),

time: 40.8 us -> 40.8 us (level)
  no operation moved by 1% of the time
where the time goes in v5:
time: 40.8 us; the launch traced here: 40.7 us
  Pallas kernels  40.1 us (98%)
  between operations  0.64 us (2%)
    pallas_call x1, Pallas kernels, shards(): pl.pallas_call(main_kernel, out_shape=tuple((pltpu.VMEM(*s) for s in (hid...  39.1 us
    pallas_call x1, Pallas kernels, shards(): pl.pallas_call(close_kernel, out_shape=tuple((jax.ShapeDtypeStruct(*s) fo...  0.99 us

profile of v5, /device:TPU:1, one launch (start us, length us, event | category | flops | bytes accessed | tf_op | source)
XLA Modules:
  0.0 40.7 jit_solution(9971347435586546817)
XLA Ops:
  0.6 39.1 %shard_map.166 = (bf16[2,24,5120]{2,1,0:T(8,128)(2,1)S(1)}, f32[2,24,128]{2,1,0:T(8,128)S(1)}, f32[1,5120]{1,0:T(1,128)S(1)}, bf16[2,2,24,128]{3,2,1,0:T(8,128)(2,1)S(1)}) custom-call(bf16[2,24,5120]{2,1,0:T(8,128)(2,1)} %tok_in.1, f32[1,5120]{1,0:T(1,128)} %bitcast.7, f32[1,5120]{1,0:T(1,128)} %bitcast.8, bf16[5120,256]{1,0:T(8,128)(2,1)} %wq_in.1, ...), custom_call_target="tpu_custom_call" | custom-call | tf_op jit(solution)/shard_map/pallas_call | solution.py:579
  39.7 1.0 %shard_map.167 = (bf16[2,24,5120]{2,1,0:T(8,128)(2,1)}, bf16[2,24,5120]{2,1,0:T(8,128)(2,1)}, bf16[2,2,24,128]{3,2,1,0:T(8,128)(2,1)}) custom-call(bf16[2,24,5120]{2,1,0:T(8,128)(2,1)S(1)} %get-tuple-element.7.hid, f32[2,24,128]{2,1,0:T(8,128)S(1)} %get-tuple-element.8.sq, f32[1,5120]{1,0:T(1,128)S(1)} %get-tuple-element.9.gain, ...), custom_call_target="tpu_custom_call" | custom-call | tf_op jit(solution)/shard_map/pallas_call | solution.py:588
